TPU v7x, 32 devices: a whole 2x2x4 slice. The times are simulated.
32 devices in a mesh: section: 2 (over x), dp: 16 (over z, y, core).
Axes of the slice: x: 2, y: 2, z: 4, core: 2. Of those that a mesh axis runs over, the one named last changes fastest.
Arguments:
- cells: float32 [32, 24, 19, 512], P('dp'), may hold values from -6 to 6
- missing_mask: int32 [32, 24, 19], P('dp'), may hold values 0 or 1
- missing_embed: float32 [512], replicated, may hold values from -6 to 6
- context_rows: int32 [32], P('dp'), may hold values from 2 to 24
- norm_gains: float32 [2, 3, 512], P('section'), may hold values from 0.25 to 1.75
- attn_in: float32 [2, 2, 512, 1536], P('section'), may hold values from -0.375 to 0.375
- attn_out: float32 [2, 2, 512, 512], P('section'), may hold values from -0.75 to 0.75
- mlp_up: float32 [2, 512, 2048], P('section'), may hold values from -0.25 to 0.25
- mlp_down: float32 [2, 2048, 512], P('section'), may hold values from -0.1875 to 0.1875
- cotangent: float32 [32, 24, 19, 512], P('dp'), may hold values from -6 to 6
Outputs:
- layer_outputs: float32 [2, 32, 24, 19, 512], P('section', 'dp')
- input_grads: float32 [2, 32, 24, 19, 512], P('section', 'dp')
- gain_grads: float32 [2, 3, 512], P('section')
- attn_in_grads: float32 [2, 2, 512, 1536], P('section')
- attn_out_grads: float32 [2, 2, 512, 512], P('section')
- up_grads: float32 [2, 512, 2048], P('section')
- down_grads: float32 [2, 2048, 512], P('section')
- missing_grad: float32 [512], replicated
Inputs may be any that keep to these rules, and one draw needn't show every extreme that they name: Only the first context_rows rows of a table are attended to in column attention; every row attends to them.
All inputs are finite; a program needn't handle non-finite values. No bound on the sum of `missing_mask` on one device may be relied on, other than what follows from the above.
Results may differ from a plain program's by a relative error of at most 0.0003.
Values sent between devices are 32-bit elements; how exact they have to be, the bound alone decides.
A program may use at most 192 MiB of HBM per device.

v0:
```python
import jax
import jax.numpy as jnp
from jax import lax
from jax.sharding import PartitionSpec as P

HEADS = 4


epsilon = 1e-05
exact_mode = lax.Precision.HIGHEST


def shifted(value, axis, steps):
    count = lax.axis_size(axis)
    first, last = (max(0, -steps), min(count, count - steps))
    return lax.ppermute(value, axis, [(source, source + steps) for source in range(first, last)])


def layer_norm(hidden, gain):
    centred = hidden - jnp.mean(hidden, axis=-1, keepdims=True)
    spread = jnp.mean(centred * centred, axis=-1, keepdims=True)
    return centred * lax.rsqrt(spread + epsilon) * gain


def project(inputs, matrix):
    return jnp.einsum("rfd,de->rfe", inputs, matrix, precision=exact_mode)


def split_heads(packed, which):
    model_width = packed.shape[2] // 3
    part = packed[:, :, which * model_width : (which + 1) * model_width]
    return part.reshape(packed.shape[0], packed.shape[1], HEADS, model_width // HEADS)


def row_attention(normed, w_in, w_out):
    packed = project(normed, w_in)
    query_part = split_heads(packed, 0)
    key_part = split_heads(packed, 1)
    value_part = split_heads(packed, 2)
    factor = query_part.shape[3] ** (-0.5)
    scores = jnp.einsum("rfhd,rghd->rhfg", query_part, key_part, precision=exact_mode) * factor
    weights = jax.nn.softmax(scores, axis=-1)
    blended = jnp.einsum("rhfg,rghd->rfhd", weights, value_part, precision=exact_mode)
    return project(blended.reshape(normed.shape), w_out)


def column_attention(normed, context, w_in, w_out):
    packed = project(normed, w_in)
    query_part = split_heads(packed, 0)
    key_part = split_heads(packed, 1)
    value_part = split_heads(packed, 2)
    factor = query_part.shape[3] ** (-0.5)
    scores = jnp.einsum("rfhd,sfhd->fhrs", query_part, key_part, precision=exact_mode) * factor
    usable = jnp.arange(normed.shape[0]) < context
    scores = jnp.where(usable, scores, -1e30)
    weights = jax.nn.softmax(scores, axis=-1)
    blended = jnp.einsum("fhrs,sfhd->rfhd", weights, value_part, precision=exact_mode)
    return project(blended.reshape(normed.shape), w_out)


def attention_part(hidden, context, gains, w_in, w_out):
    first = hidden + row_attention(layer_norm(hidden, gains[0]), w_in[0], w_out[0])
    return first + column_attention(layer_norm(first, gains[1]), context, w_in[1], w_out[1])


def feed_forward(hidden, gains, w_up, w_down):
    normed = layer_norm(hidden, gains[2])
    inner = jax.nn.gelu(project(normed, w_up), approximate=False)
    return hidden + project(inner, w_down)


def whole_layer(hidden, context, gains, w_in, w_out, w_up, w_down):
    return feed_forward(attention_part(hidden, context, gains, w_in, w_out), gains, w_up, w_down)


def backward_mlp(entering, context, grad_out, params):

    def attn_fn(hidden, gains, w_in, w_out):
        return attention_part(hidden, context, gains, w_in, w_out)

    middle, attn_back = jax.vjp(attn_fn, entering, params[0], params[1], params[2])
    _, mlp_back = jax.vjp(feed_forward, middle, params[0], params[3], params[4])
    return (attn_back, mlp_back(grad_out))


def backward_whole(entering, context, grad_out, params):
    attn_back, mlp_terms = backward_mlp(entering, context, grad_out, params)
    d_enter, gain_term, in_term, out_term = attn_back(mlp_terms[0])
    return (d_enter, (gain_term + mlp_terms[1], in_term, out_term, mlp_terms[2], mlp_terms[3]))


def local(
    cells,
    missing_mask,
    missing_embed,
    context_rows,
    norm_gains,
    attn_in,
    attn_out,
    mlp_up,
    mlp_down,
    cotangent,
):
    section_at = lax.axis_index("section")
    final_section = lax.axis_size("section") - 1
    table_count = cells.shape[0]
    params = (norm_gains[0], attn_in[0], attn_out[0], mlp_up[0], mlp_down[0])
    masked = (missing_mask == 1)[..., None]
    filled = jnp.where(masked, missing_embed, cells)
    blank_cell = jnp.zeros(cells.shape[1:], jnp.float32)
    blank_grads = tuple((jnp.zeros_like(param) for param in params))

    def forward_moment(received, moment):
        table_slot = moment - section_at
        usable = (table_slot >= 0) & (table_slot < table_count)
        chosen = jnp.clip(table_slot, 0, table_count - 1)
        entering = jnp.where(section_at == 0, filled[chosen], received)
        leaving = lax.cond(
            usable, lambda: whole_layer(entering, context_rows[chosen], *params), lambda: blank_cell
        )
        passed = shifted(leaving, "section", 1)
        return (passed, (entering, leaving))

    _, (entered, produced) = lax.scan(
        forward_moment, blank_cell, jnp.arange(table_count + final_section)
    )
    kept_inputs = lax.dynamic_slice_in_dim(entered, section_at, table_count, 0)
    layer_out = lax.dynamic_slice_in_dim(produced, section_at, table_count, 0)
    offset = final_section - section_at

    def locate(moment):
        table_slot = moment - offset
        usable = (table_slot >= 0) & (table_slot < table_count)
        return (usable, jnp.clip(table_slot, 0, table_count - 1))

    def backward_moment(carry, moment):
        received, totals = carry
        usable, chosen = locate(moment)
        grad_out = jnp.where(section_at == final_section, cotangent[chosen], received)
        d_enter, terms = lax.cond(
            usable,
            lambda: backward_whole(kept_inputs[chosen], context_rows[chosen], grad_out, params),
            lambda: (blank_cell, blank_grads),
        )
        totals = tuple((total + term for total, term in zip(totals, terms)))
        passed = shifted(d_enter, "section", -1)
        return ((passed, totals), d_enter)

    moment_count = table_count + final_section
    (_, totals), d_all = lax.scan(
        backward_moment, (blank_cell, blank_grads), jnp.arange(moment_count)
    )
    summed = lax.psum((totals[0], totals[1], totals[2], totals[3], totals[4]), "dp")
    d_inputs = lax.dynamic_slice_in_dim(d_all, offset, table_count, 0)
    is_first = section_at == 0
    partial_missing = jnp.where(
        is_first, jnp.sum(jnp.where(masked, d_inputs, 0.0), axis=(0, 1, 2)), 0.0
    )
    input_grad = jnp.where(is_first & masked, 0.0, d_inputs)
    missing_grad = lax.psum(partial_missing, ("section", "dp"))
    return (
        layer_out[None],
        input_grad[None],
        summed[0][None],
        summed[1][None],
        summed[2][None],
        summed[3][None],
        summed[4][None],
        missing_grad,
    )


def solution(mesh):
    in_specs = (
        P("dp", None, None, None),
        P("dp", None, None),
        P(),
        P("dp"),
        P("section", None, None),
        P("section", None, None, None),
        P("section", None, None, None),
        P("section", None, None),
        P("section", None, None),
        P("dp", None, None, None),
    )
    out_specs = (
        P("section", "dp", None, None, None),
        P("section", "dp", None, None, None),
        P("section", None, None),
        P("section", None, None, None),
        P("section", None, None, None),
        P("section", None, None),
        P("section", None, None),
        P(),
    )
    return jax.shard_map(local, mesh=mesh, in_specs=in_specs, out_specs=out_specs, check_vma=False)
```

profile of v0, /device:TPU:0, one launch (start us, length us, event | category | flops | bytes accessed | tf_op | source)
XLA Modules:
  0.0 1250.6 jit_solution(14955659661586731969)
XLA Ops:
  17.7 314.3 %while.40 = (s32[]{:T(128)}, f32[24,19,512]{2,0,1:T(8,128)}, f32[3,24,19,512]{3,1,2,0:T(8,128)}, f32[3,24,19,512]{3,1,2,0:T(8,128)}, s32[3]{0:T(128)S(1)}, /*ind...) while((s32[]{:T(128)}, f32[24,19,512]{2,0,1:T(8,128)}, ...), condition=%wide.region_13.14_spmd, body=%wide.region_0.13_spmd.sunk | while | flops 23278686208 | bytes 128794144 | solution.py:124
  21.6 76.0 %conditional.5 = (f32[24,19,512]{2,0,1:T(8,128)}, f32[1,24,19,512]{3,1,2,0:T(8,128)}) conditional(s32[]{:T(128)} %convert_element_type.12, () %tuple.124, (f32[24,19,512]{2,0,1:T(8,128)S(1)}, f32[3,512]{1,0:T(4,128)S(1)}, f32[2,512,1536]{2,1,0:T(8,128)}, f32[2,512,512]{2,1,0:T(8,128)S(1)}, s32[]{:T(128)}, /*index=5*/s32[2]{0:T(128)S(1)}, ...), branch_computations={%region_1.1_spmd, %region_2.12_spmd} | conditional | flops 23278452736 | bytes 115718312 | solution.py:118
  69.5 7.8 convert_reduce_fusion
  79.6 15.5 %fusion.95 = f32[24,19,512]{2,0,1:T(8,128)} fusion(f32[24,19,512]{2,0,1:T(8,128)S(1)} %get-tuple-element.658, f32[2048,512]{1,0:T(8,128)S(1)} %copy-done.17, pred[24,19,2048]{2,0,1:T(8,128)(4,1)S(1)} %and_convert_fusion.2, pred[24,19,2048]{2,0,1:T(8,128)(4,1)S(1)} %get-tuple-element.661, pred[24,19,2048]{2,0,1:T(8,128)(4,1)S(1)} %get-tuple-element.660, ...), kind=kOutput, calls=%fused_computation.114 | convolution fusion | flops 5795008512 | bytes 12599296 | tf_op jit(solution)/shard_map/while/body/eval_jaxpr/cond/branch_1_fun/rfd,de->rfe/dot_general | solution.py:26
  101.1 18.9 %collective-permute-done = f32[24,19,512]{2,0,1:T(8,128)S(1)} collective-permute-done((f32[24,19,512]{2,0,1:T(8,128)}, f32[24,19,512]{2,0,1:T(8,128)S(1)}, u32[]{:S(2)}, u32[]{:S(2)}) %collective-permute-start) | collective-permute-done | bytes 933920 | tf_op jit(solution)/shard_map/while/body/eval_jaxpr/ppermute | solution.py:16
  124.8 75.8 %conditional.5 = (f32[24,19,512]{2,0,1:T(8,128)}, f32[1,24,19,512]{3,1,2,0:T(8,128)}) conditional(s32[]{:T(128)} %convert_element_type.12, () %tuple.124, (f32[24,19,512]{2,0,1:T(8,128)S(1)}, f32[3,512]{1,0:T(4,128)S(1)}, f32[2,512,1536]{2,1,0:T(8,128)}, f32[2,512,512]{2,1,0:T(8,128)S(1)}, s32[]{:T(128)}, /*index=5*/s32[2]{0:T(128)S(1)}, ...), branch_computations={%region_1.1_spmd, %region_2.12_spmd} | conditional | flops 23278452736 | bytes 115718312 | solution.py:118
  182.5 15.5 %fusion.95 = f32[24,19,512]{2,0,1:T(8,128)} fusion(f32[24,19,512]{2,0,1:T(8,128)S(1)} %get-tuple-element.658, f32[2048,512]{1,0:T(8,128)S(1)} %copy-done.17, pred[24,19,2048]{2,0,1:T(8,128)(4,1)S(1)} %and_convert_fusion.2, pred[24,19,2048]{2,0,1:T(8,128)(4,1)S(1)} %get-tuple-element.661, pred[24,19,2048]{2,0,1:T(8,128)(4,1)S(1)} %get-tuple-element.660, ...), kind=kOutput, calls=%fused_computation.114 | convolution fusion | flops 5795008512 | bytes 12599296 | tf_op jit(solution)/shard_map/while/body/eval_jaxpr/cond/branch_1_fun/rfd,de->rfe/dot_general | solution.py:26
  207.3 18.1 %collective-permute-done = f32[24,19,512]{2,0,1:T(8,128)S(1)} collective-permute-done((f32[24,19,512]{2,0,1:T(8,128)}, f32[24,19,512]{2,0,1:T(8,128)S(1)}, u32[]{:S(2)}, u32[]{:S(2)}) %collective-permute-start) | collective-permute-done | bytes 933920 | tf_op jit(solution)/shard_map/while/body/eval_jaxpr/ppermute | solution.py:16
  236.0 74.5 %collective-permute-start = (f32[24,19,512]{2,0,1:T(8,128)}, f32[24,19,512]{2,0,1:T(8,128)S(1)}, u32[]{:S(2)}, u32[]{:S(2)}) collective-permute-start(f32[24,19,512]{2,0,1:T(8,128)} %get-tuple-element.889), channel_id=1, source_target_pairs={{0,16},{1,17},{2,18},{3,19},{4,20},{5,21},{6,22},{7,23},{8,24},{9,... | collective-permute-start | bytes 2801672 | tf_op jit(solution)/shard_map/while/body/eval_jaxpr/ppermute | solution.py:16
  312.7 17.2 %collective-permute-done = f32[24,19,512]{2,0,1:T(8,128)S(1)} collective-permute-done((f32[24,19,512]{2,0,1:T(8,128)}, f32[24,19,512]{2,0,1:T(8,128)S(1)}, u32[]{:S(2)}, u32[]{:S(2)}) %collective-permute-start) | collective-permute-done | bytes 933920 | tf_op jit(solution)/shard_map/while/body/eval_jaxpr/ppermute | solution.py:16
  335.7 589.5 %while.41 = (s32[]{:T(128)}, f32[24,19,512]{2,0,1:T(8,128)S(1)}, f32[3,512]{1,0:T(4,128)S(1)}, f32[2,512,1536]{2,1,0:T(8,128)}, f32[2,512,512]{2,1,0:T(8,128)}, ...) while((s32[]{:T(128)}, f32[24,19,512]{2,0,1:T(8,128)S(1)}, ...), condition=%wide.region_38.39_spmd.clone, body=%wide.region_14.38_spmd.clone.sunk | while | flops 63971164160 | bytes 560810240 | solution.py:150
  342.9 17.2 %conditional.6 = (f32[24,19,512]{2,0,1:T(8,128)}, f32[3,512]{1,0:T(4,128)S(1)}, f32[2,512,1536]{2,1,0:T(8,128)}, f32[2,512,512]{2,1,0:T(8,128)}, f32[512,2048]{1...) conditional(s32[]{:T(128)} %convert_element_type.13, () %tuple.127, (pred[]{:T(512)}, s32[]{:T(128)}, ...), branch_computations={%region_15.15_spmd, %region_16.37_spmd} | conditional | flops 63962771456 | bytes 393707168 | solution.py:140
  382.7 150.4 %collective-permute-done.1 = f32[24,19,512]{2,0,1:T(8,128)S(1)} collective-permute-done((f32[24,19,512]{2,0,1:T(8,128)}, f32[24,19,512]{2,0,1:T(8,128)S(1)}, u32[]{:S(2)}, u32[]{:S(2)}) %collective-permute-start.1) | collective-permute-done | bytes 933920 | tf_op jit(solution)/shard_map/while/body/eval_jaxpr/ppermute | solution.py:16
  534.5 167.5 %conditional.6 = (f32[24,19,512]{2,0,1:T(8,128)}, f32[3,512]{1,0:T(4,128)S(1)}, f32[2,512,1536]{2,1,0:T(8,128)}, f32[2,512,512]{2,1,0:T(8,128)}, f32[512,2048]{1...) conditional(s32[]{:T(128)} %convert_element_type.13, () %tuple.127, (pred[]{:T(512)}, s32[]{:T(128)}, ...), branch_computations={%region_15.15_spmd, %region_16.37_spmd} | conditional | flops 63962771456 | bytes 393707168 | solution.py:140
  588.9 8.4 fusion.176
  604.8 8.8 fusion.185
  620.9 9.0 convolution_bitcast_fusion.2
  729.6 167.4 %conditional.6 = (f32[24,19,512]{2,0,1:T(8,128)}, f32[3,512]{1,0:T(4,128)S(1)}, f32[2,512,1536]{2,1,0:T(8,128)}, f32[2,512,512]{2,1,0:T(8,128)}, f32[512,2048]{1...) conditional(s32[]{:T(128)} %convert_element_type.13, () %tuple.127, (pred[]{:T(512)}, s32[]{:T(128)}, ...), branch_computations={%region_15.15_spmd, %region_16.37_spmd} | conditional | flops 63962771456 | bytes 393707168 | solution.py:140
  783.8 8.4 fusion.176
  799.7 8.8 fusion.185
  815.8 9.0 convolution_bitcast_fusion.2
  928.6 42.3 %psum.47 = f32[512]{0:T(512)} all-reduce(f32[512]{0:T(512)S(1)} %broadcast_select_fusion.1), channel_id=1, replica_groups=mesh['section'=2,'dp'=16] {'section','dp'}, use_global_device_ids=true, to_apply=%region_45.46 | all-reduce | flops 512 | bytes 4096 | tf_op jit(solution)/shard_map/psum | solution.py:160
  971.0 34.8 %psum.42 = f32[1,3,512]{2,0,1:T(1,128)} all-reduce(f32[1,3,512]{2,0,1:T(1,128)S(1)} %broadcast_in_dim.253), channel_id=1, replica_groups=mesh['section'=2,'dp'=16] {'dp'}, use_global_device_ids=true, to_apply=%region_39.40 | all-reduce | flops 1536 | bytes 12288 | tf_op jit(solution)/shard_map/psum | solution.py:153
  1008.7 220.2 %all-reduce.16.cloned.1.call-done = (f32[1,2,512,1536]{3,2,1,0:T(8,128)}, f32[1,2,512,512]{3,2,1,0:T(8,128)}, f32[1,512,2048]{2,1,0:T(8,128)}, f32[1,2048,512]{2,1,0:T(8,128)}) async-done(((f32[1,2,512,1536]{3,2,1,0:T(8,128)}, f32[1,2,512,512]{3,2,1,0:T(8,128)}, f32[1,512,2048]{2,1,0:T(8,128)}, f32[1,2048,512]{2,1,0:T(8,128)}), (f32[1,2,512,1536]{3,2,1,0:T(8,128)}, f32[1,2,512,512]{3,2,1,0:T(8,128)}, ...) | async-done | bytes 16777232 | tf_op jit(solution)/shard_map/psum | solution.py:153
  (469 shorter events, 548.0 us)
Async XLA Ops:
  7.2 1221.7 %all-reduce.16.cloned.1.call-start = ((), (), s32[]{:S(2)}) async-start(), calls=%async_computation | async-start | bytes 33554432 | tf_op jit(solution)/shard_map/psum | solution.py:153
  69.5 10.0 copy-start.17
  97.6 22.5 %collective-permute-start = (f32[24,19,512]{2,0,1:T(8,128)}, f32[24,19,512]{2,0,1:T(8,128)S(1)}, u32[]{:S(2)}, u32[]{:S(2)}) collective-permute-start(f32[24,19,512]{2,0,1:T(8,128)} %get-tuple-element.889), channel_id=1, source_target_pairs={{0,16},{1,17},{2,18},{3,19},{4,20},{5,21},{6,22},{7,23},{8,24},{9,... | collective-permute-start | bytes 2801672 | tf_op jit(solution)/shard_map/while/body/eval_jaxpr/ppermute | solution.py:16
  172.5 10.0 copy-start.17
  200.6 24.8 %collective-permute-start = (f32[24,19,512]{2,0,1:T(8,128)}, f32[24,19,512]{2,0,1:T(8,128)S(1)}, u32[]{:S(2)}, u32[]{:S(2)}) collective-permute-start(f32[24,19,512]{2,0,1:T(8,128)} %get-tuple-element.889), channel_id=1, source_target_pairs={{0,16},{1,17},{2,18},{3,19},{4,20},{5,21},{6,22},{7,23},{8,24},{9,... | collective-permute-start | bytes 2801672 | tf_op jit(solution)/shard_map/while/body/eval_jaxpr/ppermute | solution.py:16
  236.0 93.8 %collective-permute-start = (f32[24,19,512]{2,0,1:T(8,128)}, f32[24,19,512]{2,0,1:T(8,128)S(1)}, u32[]{:S(2)}, u32[]{:S(2)}) collective-permute-start(f32[24,19,512]{2,0,1:T(8,128)} %get-tuple-element.889), channel_id=1, source_target_pairs={{0,16},{1,17},{2,18},{3,19},{4,20},{5,21},{6,22},{7,23},{8,24},{9,... | collective-permute-start | bytes 2801672 | tf_op jit(solution)/shard_map/while/body/eval_jaxpr/ppermute | solution.py:16
  360.2 172.9 %collective-permute-start.1 = (f32[24,19,512]{2,0,1:T(8,128)}, f32[24,19,512]{2,0,1:T(8,128)S(1)}, u32[]{:S(2)}, u32[]{:S(2)}) collective-permute-start(f32[24,19,512]{2,0,1:T(8,128)} %get-tuple-element.911), channel_id=1, source_target_pairs={{16,0},{17,1},{18,2},{19,3},{20,4},{21,5},{22,6},{23,7},{24,8},{25... | collective-permute-start | bytes 2801672 | tf_op jit(solution)/shard_map/while/body/eval_jaxpr/ppermute | solution.py:16
  382.7 150.4 %copy-start.4 = (f32[2,512,1536]{2,1,0:T(8,128)}, f32[2,512,1536]{2,1,0:T(8,128)S(1)}, u32[]{:S(2)}) copy-start(f32[2,512,1536]{2,1,0:T(8,128)S(1)} %select_add_fusion.11) | copy-start | bytes 18874372 | tf_op jit(solution)/shard_map/while
  588.9 8.4 copy-start.5
  588.9 8.4 copy-start.18
  620.8 9.0 copy-start.22
  647.9 8.7 copy-start.6
  648.0 7.0 copy-start.21
  648.0 8.7 copy-start.23
  681.4 8.2 copy-start.7
  702.0 25.4 %collective-permute-start.1 = (f32[24,19,512]{2,0,1:T(8,128)}, f32[24,19,512]{2,0,1:T(8,128)S(1)}, u32[]{:S(2)}, u32[]{:S(2)}) collective-permute-start(f32[24,19,512]{2,0,1:T(8,128)} %get-tuple-element.911), channel_id=1, source_target_pairs={{16,0},{17,1},{18,2},{19,3},{20,4},{21,5},{22,6},{23,7},{24,8},{25... | collective-permute-start | bytes 2801672 | tf_op jit(solution)/shard_map/while/body/eval_jaxpr/ppermute | solution.py:16
  783.8 8.4 copy-start.5
  783.8 8.4 copy-start.18
  815.8 9.0 copy-start.22
  842.9 8.7 copy-start.6
  842.9 7.0 copy-start.21
  842.9 8.7 copy-start.23
  876.3 8.2 copy-start.7
  896.9 23.2 %collective-permute-start.1 = (f32[24,19,512]{2,0,1:T(8,128)}, f32[24,19,512]{2,0,1:T(8,128)S(1)}, u32[]{:S(2)}, u32[]{:S(2)}) collective-permute-start(f32[24,19,512]{2,0,1:T(8,128)} %get-tuple-element.911), channel_id=1, source_target_pairs={{16,0},{17,1},{18,2},{19,3},{20,4},{21,5},{22,6},{23,7},{24,8},{25... | collective-permute-start | bytes 2801672 | tf_op jit(solution)/shard_map/while/body/eval_jaxpr/ppermute | solution.py:16
  (65 other events, 239.8 us)
Sparse Core Ops, SparseCore 0:
  925.4 303.3 all-reduce.15
where the time goes:
time: 1250 us
  waiting for transfers between devices  427 us (34%)
  matrix products  346 us (28%)
  local copies, waits for them, and re-layouts  154 us (12%)
  other arithmetic  122 us (10%)
  starting transfers between devices  84.2 us (7%)
  blocking collectives  77.1 us (6%)
  loops' own time  26.8 us (2%)
  between operations  14.4 us (1%)
    dot_general x46, matrix products, project(): return jnp.einsum('rfd,de->rfe', inputs, matrix, precision=exact_mode)  261 us
    psum x1, waiting for transfers between devices, local(): lax.psum((totals[0], totals[1], totals[2], totals[3], totals[4]), 'dp')  220 us
    ppermute x6, waiting for transfers between devices, shifted(): lax.ppermute(value, axis, [(source, source + steps) for source in range(f...  207 us
    ppermute x6, starting transfers between devices, shifted(): lax.ppermute(value, axis, [(source, source + steps) for source in range(f...  84.2 us
    add x15, other arithmetic, backward_moment(): totals = tuple((total + term for total, term in zip(totals, terms)))  56.9 us
    psum x1, blocking collectives, local(): missing_grad = lax.psum(partial_missing, ('section', 'dp'))  42.3 us
    reshape x24, local copies, waits for them, and re-layouts, split_heads(): part.reshape(packed.shape[0], packed.shape[1], HEADS, model_width // HEADS)  39.8 us
    psum x1, blocking collectives, local(): lax.psum((totals[0], totals[1], totals[2], totals[3], totals[4]), 'dp')  34.8 us
  transfers between devices with their start and end apart: 7, of which 6 were waited for; matrix products, arithmetic and copies ran while one was open for 6% of the time, Pallas kernels for 0%

commit v1 on v0

v1 whole, which is shorter than its diff:
```python
import functools

import jax
import jax.numpy as jnp
from jax import lax
from jax.experimental import pallas as pl
from jax.experimental.pallas import tpu as pltpu
from jax.sharding import PartitionSpec as P

HEADS = 4
EPSILON = 1e-05
NEG = -1e30
INV_SQRT2 = 0.7071067811865476
INV_SQRT2PI = 0.3989422804014327
PREC = lax.Precision.HIGH
VMEM_LIMIT = 62 * 1024 * 1024


def mm(a, b):
    return lax.dot_general(a, b, (((1,), (0,)), ((), ())), precision=PREC, preferred_element_type=jnp.float32)


def mm_nt(a, b):
    return lax.dot_general(a, b, (((1,), (1,)), ((), ())), precision=PREC, preferred_element_type=jnp.float32)


def mm_tn(a, b):
    return lax.dot_general(a, b, (((0,), (0,)), ((), ())), precision=PREC, preferred_element_type=jnp.float32)


def normalized(h):
    centred = h - jnp.mean(h, axis=-1, keepdims=True)
    rstd = lax.rsqrt(jnp.mean(centred * centred, axis=-1, keepdims=True) + EPSILON)
    return centred * rstd, rstd


def norm_back(h, gain, da):
    n, rstd = normalized(h)
    dgain = jnp.sum(da * n, axis=0, keepdims=True)
    dn = da * gain
    dh = rstd * (dn - jnp.mean(dn, axis=-1, keepdims=True) - n * jnp.mean(dn * n, axis=-1, keepdims=True))
    return dh, n * gain, dgain


def cell_ids(start, count, feat, along):
    shape = (count, 1) if along == 0 else (1, count)
    at = lax.broadcasted_iota(jnp.int32, shape, along) + start
    mult = (1 << 20) // feat + 1
    row = lax.shift_right_logical(at * mult, 20)
    return row, at - row * feat


def row_blocks(rows, feat):
    cells = rows * feat
    half = ((rows // 2) * feat + 7) // 8 * 8
    first_keys = min(cells, ((((half - 1) // feat) + 1) * feat + 7) // 8 * 8)
    second_keys = ((half // feat) * feat) // 8 * 8
    return (((0, half), (0, first_keys)), ((half, cells), (second_keys, cells)))


def probs(q, k, mask, scale):
    s = jnp.where(mask, mm_nt(q, k) * scale, NEG)
    e = jnp.exp(s - jnp.max(s, axis=-1, keepdims=True))
    return e / jnp.sum(e, axis=-1, keepdims=True)


def row_mask(block, feat):
    (q0, q1), (k0, k1) = block
    return cell_ids(q0, q1 - q0, feat, 0)[0] == cell_ids(k0, k1 - k0, feat, 1)[0]


def col_mask(cells, feat, context):
    key_row, key_feat = cell_ids(0, cells, feat, 1)
    return (cell_ids(0, cells, feat, 0)[1] == key_feat) & (key_row < context)


def lanes(j, width):
    return pl.ds(pl.multiple_of(j * width, width), width)


def start(src, dst, sem):
    copy = pltpu.make_async_copy(src, dst, sem)
    copy.start()
    return copy


def fwd_kernel(rows, feat, first, *refs):
    ctl, ctx, x_hbm, gains, win, wout, wup, wdown = refs[:8]
    refs = refs[8:] if first else refs[12:]
    y_hbm, hs, qkvs, os, zs = refs[:5]
    win_v, wout_v, wup_v, wdown_v, h_v, qkv_v, o_v, z_v, g_v, a_v, y_v, sem_in, sem_out = refs[5:]
    cells, width = a_v.shape
    ff = z_v.shape[1]
    hd = width // HEADS
    scale = hd ** (-0.5)
    tile = 256

    @pl.when(ctl[0] == 1)
    def _():
        table = ctl[1]
        c_x = start(x_hbm, h_v.at[0], sem_in.at[0])
        c_win0 = start(win.at[0], win_v.at[0], sem_in.at[1])
        c_wout0 = start(wout.at[0], wout_v.at[0], sem_in.at[2])
        c_win1 = start(win.at[1], win_v.at[1], sem_in.at[3])
        c_wout1 = start(wout.at[1], wout_v.at[1], sem_in.at[4])
        c_up = start(wup, wup_v, sem_in.at[5])
        c_down = start(wdown, wdown_v, sem_in.at[6])
        outs = []
        c_x.wait()
        outs.append(start(h_v.at[0], hs.at[table, 0], sem_out.at[0]))
        for site in range(2):
            a_v[...] = normalized(h_v[site])[0] * gains[site : site + 1, :]
            (c_win0, c_win1)[site].wait()

            @pl.loop(0, 3 * width // tile)
            def _(j):
                qkv_v[site, :, lanes(j, tile)] = mm(a_v[...], win_v[site, :, lanes(j, tile)])

            outs.append(start(qkv_v.at[site], qkvs.at[table, site], sem_out.at[1 + site]))
            if site == 0:
                blocks = row_blocks(rows, feat)
                masks = [row_mask(block, feat) for block in blocks]
            else:
                blocks = (((0, cells), (0, cells)),)
                masks = [col_mask(cells, feat, ctx[table])]

            @pl.loop(0, HEADS)
            def _(head):
                for ((q0, q1), (k0, k1)), mask in zip(blocks, masks):
                    q = qkv_v[site, q0:q1, lanes(head, hd)]
                    k = qkv_v[site, k0:k1, lanes(HEADS + head, hd)]
                    v = qkv_v[site, k0:k1, lanes(2 * HEADS + head, hd)]
                    o_v[site, q0:q1, lanes(head, hd)] = mm(probs(q, k, mask, scale), v)

            outs.append(start(o_v.at[site], os.at[table, site], sem_out.at[3 + site]))
            (c_wout0, c_wout1)[site].wait()

            @pl.loop(0, width // tile)
            def _(j):
                at = lanes(j, tile)
                h_v[site + 1, :, at] = h_v[site, :, at] + mm(o_v[site], wout_v[site, :, at])

            outs.append(start(h_v.at[site + 1], hs.at[table, site + 1], sem_out.at[5 + site]))
        a_v[...] = normalized(h_v[2])[0] * gains[2:3, :]
        c_up.wait()

        @pl.loop(0, ff // tile)
        def _(j):
            at = lanes(j, tile)
            z = mm(a_v[...], wup_v[:, at])
            z_v[:, at] = z
            g_v[:, at] = 0.5 * z * (1.0 + lax.erf(z * INV_SQRT2))

        outs.append(start(z_v, zs.at[table], sem_out.at[7]))
        c_down.wait()

        @pl.loop(0, width // tile)
        def _(j):
            at = lanes(j, tile)
            y_v[:, at] = h_v[2, :, at] + mm(g_v[...], wdown_v[:, at])

        outs.append(start(y_v, y_hbm, sem_out.at[8]))
        for copy in outs:
            copy.wait()


def bwd_kernel(rows, feat, first, *refs):
    ctl, ctx, dy_a, dy_b, gains, win, wout, wup, wdown, hs, qkvs, zs = refs[:12]
    refs = refs[12:] if first else refs[17:]
    dx_hbm, dgain, as_, dqkvs, dhs, gs, dzs = refs[:7]
    win_v, wout_v, wup_v, wdown_v, h_v, qkv_v, z_v, a_v, dqkv_v, dh_v, g_v, do_v, sem_in, sem_out = refs[7:]
    cells, width = do_v.shape
    ff = z_v.shape[1]
    hd = width // HEADS
    scale = hd ** (-0.5)
    tile = 256

    @pl.when(ctl[0] == 1)
    def _():
        table = ctl[1]

        @pl.when(ctl[2] == 0)
        def _():
            start(dy_a, dh_v.at[2], sem_in.at[0]).wait()

        @pl.when(ctl[2] == 1)
        def _():
            start(dy_b, dh_v.at[2], sem_in.at[0]).wait()

        c_down = start(wdown, wdown_v, sem_in.at[1])
        c_z = start(zs.at[table], z_v, sem_in.at[2])
        c_up = start(wup, wup_v, sem_in.at[3])
        c_h = start(hs.at[table], h_v, sem_in.at[4])
        c_wout = start(wout, wout_v, sem_in.at[5])
        c_qkv = start(qkvs.at[table], qkv_v, sem_in.at[6])
        c_win = start(win, win_v, sem_in.at[7])
        outs = []
        outs.append(start(dh_v.at[2], dhs.at[table, 2], sem_out.at[0]))
        c_down.wait()
        c_z.wait()

        @pl.loop(0, ff // tile)
        def _(j):
            at = lanes(j, tile)
            dg = mm_nt(dh_v[2], wdown_v[at, :])
            z = z_v[:, at]
            phi = 0.5 * (1.0 + lax.erf(z * INV_SQRT2))
            g_v[:, at] = z * phi
            z_v[:, at] = dg * (phi + z * (INV_SQRT2PI * jnp.exp(-0.5 * z * z)))

        outs.append(start(g_v, gs.at[table], sem_out.at[1]))
        outs.append(start(z_v, dzs.at[table], sem_out.at[2]))
        c_up.wait()

        @pl.loop(0, width // tile)
        def _(j):
            at = lanes(j, tile)
            do_v[:, at] = mm_nt(z_v[...], wup_v[at, :])

        c_h.wait()
        for site in (1, 0):
            dh, a, dg_row = norm_back(h_v[site + 1], gains[site + 1 : site + 2, :], do_v[...])
            dh_v[site] = dh_v[site + 1] + dh
            a_v[site + 1] = a
            dgain[site + 1 : site + 2, :] = dg_row
            outs.append(start(dh_v.at[site], dhs.at[table, site], sem_out.at[3 + site]))
            outs.append(start(a_v.at[site + 1], as_.at[table, site + 1], sem_out.at[5 + site]))
            if site == 1:
                c_wout.wait()

            @pl.loop(0, width // tile)
            def _(j):
                at = lanes(j, tile)
                do_v[:, at] = mm_nt(dh_v[site], wout_v[site, at, :])

            if site == 1:
                c_qkv.wait()
            if site == 0:
                blocks = row_blocks(rows, feat)
                masks = [row_mask(block, feat) for block in blocks]
            else:
                blocks = (((0, cells), (0, cells)),)
                masks = [col_mask(cells, feat, ctx[table])]

            @pl.loop(0, HEADS)
            def _(head):
                done = 0
                at_q, at_k, at_v = lanes(head, hd), lanes(HEADS + head, hd), lanes(2 * HEADS + head, hd)
                for ((q0, q1), (k0, k1)), mask in zip(blocks, masks):
                    q = qkv_v[site, q0:q1, at_q]
                    k = qkv_v[site, k0:k1, at_k]
                    v = qkv_v[site, k0:k1, at_v]
                    do = do_v[q0:q1, at_q]
                    p = probs(q, k, mask, scale)
                    dp = mm_nt(do, v)
                    ds = p * (dp - jnp.sum(p * dp, axis=-1, keepdims=True)) * scale
                    dqkv_v[site, q0:q1, at_q] = mm(ds, k)
                    for at, term in ((at_k, mm_tn(ds, q)), (at_v, mm_tn(p, do))):
                        if done > k0:
                            dqkv_v[site, k0:done, at] += term[: done - k0]
                            dqkv_v[site, done:k1, at] = term[done - k0 :]
                        else:
                            dqkv_v[site, k0:k1, at] = term
                    done = k1

            outs.append(start(dqkv_v.at[site], dqkvs.at[table, site], sem_out.at[7 + site]))
            if site == 1:
                c_win.wait()

            @pl.loop(0, width // tile)
            def _(j):
                at = lanes(j, tile)
                do_v[:, at] = mm_nt(dqkv_v[site], win_v[site, at, :])

        dh, a, dg_row = norm_back(h_v[0], gains[0:1, :], do_v[...])
        do_v[...] = dh_v[0] + dh
        a_v[0] = a
        dgain[0:1, :] = dg_row
        outs.append(start(a_v.at[0], as_.at[table, 0], sem_out.at[9]))
        outs.append(start(do_v, dx_hbm, sem_out.at[10]))
        for copy in outs:
            copy.wait()


SMEM = pl.BlockSpec(memory_space=pltpu.SMEM)
VMEM = pl.BlockSpec(memory_space=pltpu.VMEM)
ANY = pl.BlockSpec(memory_space=pl.ANY)


def f32(*shape):
    return jax.ShapeDtypeStruct(shape, jnp.float32)


def forward(rows, feat, tables, ctl, ctx, x, params, saved):
    gains, win, wout, wup, wdown = params
    cells, width = x.shape
    ff = wup.shape[1]
    first = saved is None
    operands = [ctl, ctx, x, gains, win, wout, wup, wdown]
    specs = [SMEM, SMEM, ANY, VMEM, ANY, ANY, ANY, ANY]
    aliases = {}
    if not first:
        aliases = {len(operands) + i: i + 1 for i in range(4)}
        operands += list(saved)
        specs += [ANY] * 4
    outs = pl.pallas_call(
        functools.partial(fwd_kernel, rows, feat, first),
        out_shape=(
            f32(cells, width),
            f32(tables, 3, cells, width),
            f32(tables, 2, cells, 3 * width),
            f32(tables, 2, cells, width),
            f32(tables, cells, ff),
        ),
        in_specs=specs,
        out_specs=[ANY] * 5,
        input_output_aliases=aliases,
        scratch_shapes=[
            pltpu.VMEM(win.shape, jnp.float32),
            pltpu.VMEM(wout.shape, jnp.float32),
            pltpu.VMEM(wup.shape, jnp.float32),
            pltpu.VMEM(wdown.shape, jnp.float32),
            pltpu.VMEM((3, cells, width), jnp.float32),
            pltpu.VMEM((2, cells, 3 * width), jnp.float32),
            pltpu.VMEM((2, cells, width), jnp.float32),
            pltpu.VMEM((cells, ff), jnp.float32),
            pltpu.VMEM((cells, ff), jnp.float32),
            pltpu.VMEM((cells, width), jnp.float32),
            pltpu.VMEM((cells, width), jnp.float32),
            pltpu.SemaphoreType.DMA((7,)),
            pltpu.SemaphoreType.DMA((9,)),
        ],
        compiler_params=pltpu.CompilerParams(vmem_limit_bytes=VMEM_LIMIT),
        name="layer_forward",
    )(*operands)
    return outs[0], outs[1:]


def backward(rows, feat, tables, ctl, ctx, dy_a, dy_b, params, saved, kept):
    gains, win, wout, wup, wdown = params
    cells, width = dy_a.shape
    ff = wup.shape[1]
    first = kept is None
    hs, qkvs, _, zs = saved
    operands = [ctl, ctx, dy_a, dy_b, gains, win, wout, wup, wdown, hs, qkvs, zs]
    specs = [SMEM, SMEM, ANY, ANY, VMEM, ANY, ANY, ANY, ANY, ANY, ANY, ANY]
    aliases = {}
    if not first:
        aliases = {len(operands) + i: i + 2 for i in range(5)}
        operands += list(kept)
        specs += [ANY] * 5
    outs = pl.pallas_call(
        functools.partial(bwd_kernel, rows, feat, first),
        out_shape=(
            f32(cells, width),
            f32(3, width),
            f32(tables, 3, cells, width),
            f32(tables, 2, cells, 3 * width),
            f32(tables, 3, cells, width),
            f32(tables, cells, ff),
            f32(tables, cells, ff),
        ),
        in_specs=specs,
        out_specs=[ANY, VMEM] + [ANY] * 5,
        input_output_aliases=aliases,
        scratch_shapes=[
            pltpu.VMEM(win.shape, jnp.float32),
            pltpu.VMEM(wout.shape, jnp.float32),
            pltpu.VMEM(wup.shape, jnp.float32),
            pltpu.VMEM(wdown.shape, jnp.float32),
            pltpu.VMEM((3, cells, width), jnp.float32),
            pltpu.VMEM((2, cells, 3 * width), jnp.float32),
            pltpu.VMEM((cells, ff), jnp.float32),
            pltpu.VMEM((3, cells, width), jnp.float32),
            pltpu.VMEM((2, cells, 3 * width), jnp.float32),
            pltpu.VMEM((3, cells, width), jnp.float32),
            pltpu.VMEM((cells, ff), jnp.float32),
            pltpu.VMEM((cells, width), jnp.float32),
            pltpu.SemaphoreType.DMA((8,)),
            pltpu.SemaphoreType.DMA((11,)),
        ],
        compiler_params=pltpu.CompilerParams(vmem_limit_bytes=VMEM_LIMIT),
        name="layer_backward",
    )(*operands)
    return outs[0], outs[1], outs[2:]


def local(
    cells,
    missing_mask,
    missing_embed,
    context_rows,
    norm_gains,
    attn_in,
    attn_out,
    mlp_up,
    mlp_down,
    cotangent,
):
    section = lax.axis_index("section")
    tables, rows, feat, width = cells.shape
    count = rows * feat
    params = (norm_gains[0], attn_in[0], attn_out[0], mlp_up[0], mlp_down[0])
    masked = (missing_mask == 1)[..., None]
    filled = jnp.where(masked, missing_embed, cells).reshape(tables, count, width)
    cot = cotangent.reshape(tables, count, width)
    is_first = section == 0

    def ctl(at_first, at_last):
        return jnp.where(is_first, jnp.array(at_first, jnp.int32), jnp.array(at_last, jnp.int32))

    fwd = functools.partial(forward, rows, feat, tables)
    bwd = functools.partial(backward, rows, feat, tables)
    idle = (0, 0, 0)
    fwd_pairs, bwd_pairs = [(0, 1)], [(1, 0)]

    y0, saved = fwd(ctl((1, 0, 0), idle), context_rows, filled[0], params, None)
    r0 = lax.ppermute(y0, "section", fwd_pairs)
    y1, saved = fwd(ctl((1, 1, 0), idle), context_rows, filled[1], params, saved)
    r1 = lax.ppermute(y1, "section", fwd_pairs)
    y2, saved = fwd(ctl(idle, (1, 0, 0)), context_rows, r0, params, saved)
    d0, dg0, kept = bwd(ctl(idle, (1, 0, 0)), context_rows, cot[0], cot[0], params, saved, None)
    e0 = lax.ppermute(d0, "section", bwd_pairs)
    y3, saved = fwd(ctl(idle, (1, 1, 0)), context_rows, r1, params, saved)
    d1, dg1, kept = bwd(ctl((1, 0, 1), (1, 1, 0)), context_rows, cot[1], e0, params, saved, kept)
    e1 = lax.ppermute(d1, "section", bwd_pairs)
    d2, dg2, kept = bwd(ctl((1, 1, 0), idle), context_rows, e1, e1, params, saved, kept)

    layer_out = jnp.where(is_first, jnp.stack([y0, y1]), jnp.stack([y2, y3]))
    d_inputs = jnp.where(is_first, jnp.stack([d1, d2]), jnp.stack([d0, d1]))
    d_gain = jnp.where(is_first, dg1 + dg2, dg0 + dg1)
    as_, dqkvs, dhs, gs, dzs = kept
    os = saved[2]

    def summed(a, b, spec):
        return jnp.einsum(spec, a, b, precision=PREC, preferred_element_type=jnp.float32)

    d_up = summed(as_[:, 2], dzs, "tck,tcn->kn")
    d_down = summed(gs, dhs[:, 2], "tck,tcn->kn")
    d_out = jnp.stack([summed(os[:, s], dhs[:, s], "tck,tcn->kn") for s in range(2)])
    d_in = jnp.stack([summed(as_[:, s], dqkvs[:, s], "tck,tcn->kn") for s in range(2)])

    d_inputs = d_inputs.reshape(cells.shape)
    missing = jnp.where(is_first, jnp.sum(jnp.where(masked, d_inputs, 0.0), axis=(0, 1, 2)), 0.0)
    input_grad = jnp.where(is_first & masked, 0.0, d_inputs)
    up_all, down_all = lax.psum((d_up, d_down), "dp")
    in_all, out_all, gain_all = lax.psum((d_in, d_out, d_gain), "dp")
    missing_all = lax.psum(missing, ("section", "dp"))
    return (
        layer_out.reshape(cells.shape)[None],
        input_grad[None],
        gain_all[None],
        in_all[None],
        out_all[None],
        up_all[None],
        down_all[None],
        missing_all,
    )


def solution(mesh):
    in_specs = (
        P("dp", None, None, None),
        P("dp", None, None),
        P(),
        P("dp"),
        P("section", None, None),
        P("section", None, None, None),
        P("section", None, None, None),
        P("section", None, None),
        P("section", None, None),
        P("dp", None, None, None),
    )
    out_specs = (
        P("section", "dp", None, None, None),
        P("section", "dp", None, None, None),
        P("section", None, None),
        P("section", None, None, None),
        P("section", None, None, None),
        P("section", None, None),
        P("section", None, None),
        P(),
    )
    return jax.shard_map(local, mesh=mesh, in_specs=in_specs, out_specs=out_specs, check_vma=False)
```

time: 1250 us -> 700 us (0.56)
  matrix products: 346 us -> 50.8 us
  Pallas kernels: 0 us -> 182 us
  waiting for transfers between devices: 427 us -> 307 us
  other arithmetic: 122 us -> 15 us
  local copies, waits for them, and re-layouts: 154 us -> 47.5 us
  starting transfers between devices: 84.2 us -> 7.1 us
  loops' own time: 26.8 us -> 0 us
    dot_general x78 -> x6, matrix products: 346 us -> 50.8 us  [summed(): jnp.einsum(spec, a, b, precision=PREC, preferred_element_type=jnp.float32)]
    pallas_call x0 -> x7, Pallas kernels: none -> 182 us  [the longest x3 96.6 us: backward(): pl.pallas_call(functools.partial(bwd_kernel, rows, feat, first), out_shap...]
    ppermute x6 -> x4, waiting for transfers between devices: 207 us -> 107 us  [the longest x1 70.3 us: local(): e0 = lax.ppermute(d0, 'section', bwd_pairs)]
    ppermute x6 -> x4, starting transfers between devices: 84.2 us -> 7.07 us  [the longest x1 2.25 us: local(): r0 = lax.ppermute(y0, 'section', fwd_pairs)]
    add x17 -> x0, other arithmetic: 56.9 us -> none  [the longest x15 56.9 us: backward_moment(): totals = tuple((total + term for total, term in zip(totals, terms)))]
    reshape x28 -> x0, local copies, waits for them, and re-layouts: 49.9 us -> none  [the longest x24 39.8 us: split_heads(): part.reshape(packed.shape[0], packed.shape[1], HEADS, model_width // HEADS)]
    another operation x8 -> x0, loops' own time: 26.8 us -> none  [the longest x1 11.3 us: local(): lax.scan(backward_moment, (blank_cell, blank_grads), jnp.arange(moment_co...]
    another operation x6 -> x0, other arithmetic: 21.1 us -> none  [feed_forward(): inner = jax.nn.gelu(project(normed, w_up), approximate=False)]
  transfers between devices with their start and end apart: 7 -> 5, of which waited for: 6 -> 3; matrix products, arithmetic and copies ran while one was open for 6% -> 5% of each run, Pallas kernels for 0% -> 8%
where the time goes in v1:
time: 700 us; the launch traced here: 698 us
  waiting for transfers between devices  307 us (44%)
  Pallas kernels  182 us (26%)
  blocking collectives  74.3 us (11%)
  matrix products  50.8 us (7%)
  local copies, waits for them, and re-layouts  47.5 us (7%)
  other arithmetic  15 us (2%)
  between operations  14.7 us (2%)
  starting transfers between devices  7.1 us (1%)
    psum x1, waiting for transfers between devices, local(): in_all, out_all, gain_all = lax.psum((d_in, d_out, d_gain), 'dp')  200 us
    pallas_call x3, Pallas kernels, backward(): pl.pallas_call(functools.partial(bwd_kernel, rows, feat, first), out_shap...  96.6 us
    pallas_call x4, Pallas kernels, forward(): pl.pallas_call(functools.partial(fwd_kernel, rows, feat, first), out_shap...  85.3 us
    ppermute x1, waiting for transfers between devices, local(): e0 = lax.ppermute(d0, 'section', bwd_pairs)  70.3 us
    dot_general x6, matrix products, summed(): jnp.einsum(spec, a, b, precision=PREC, preferred_element_type=jnp.float32)  50.8 us
    psum x1, blocking collectives, local(): missing_all = lax.psum(missing, ('section', 'dp'))  38.4 us
    ppermute x1, waiting for transfers between devices, local(): e1 = lax.ppermute(d1, 'section', bwd_pairs)  36.3 us
    psum x1, blocking collectives, local(): in_all, out_all, gain_all = lax.psum((d_in, d_out, d_gain), 'dp')  35.9 us
  transfers between devices with their start and end apart: 5, of which 3 were waited for; matrix products, arithmetic and copies ran while one was open for 5% of the time, Pallas kernels for 8%

profile of v1, /device:TPU:0, one launch (start us, length us, event | category | flops | bytes accessed | tf_op | source)
XLA Modules:
  0.0 698.1 jit_solution(5760928080858898337)
XLA Ops:
  8.1 2.7 copy_select_fusion
  13.2 34.5 %layer_forward.4 = (f32[456,512]{1,0:T(8,128)}, f32[2,3,456,512]{3,2,1,0:T(8,128)}, f32[2,2,456,1536]{3,2,1,0:T(8,128)}, f32[2,2,456,512]{3,2,1,0:T(8,128)}, f32[2,456,2048]{2,1,0:T(8,128)}) custom-call(s32[3]{0:T(128)} %get-tuple-element.120.refs_0_, s32[2]{0:T(128)} %refs_1_.13, f32[456,512]{1,0:T(8,128)} %squeeze.58.refs_2_, f32[3,512]{1,0:T(4,128)} %bitcast.109, ...), custom_call_target="tpu_custom_call" | custom-call | tf_op jit(solution)/shard_map/layer_forward/pallas_call | solution.py:306
  51.5 34.8 %layer_forward.5 = (f32[456,512]{1,0:T(8,128)}, f32[2,3,456,512]{3,2,1,0:T(8,128)}, f32[2,2,456,1536]{3,2,1,0:T(8,128)}, f32[2,2,456,512]{3,2,1,0:T(8,128)}, f32[2,456,2048]{2,1,0:T(8,128)}) custom-call(s32[3]{0:T(128)} %get-tuple-element.117.refs_0_, s32[2]{0:T(128)} %refs_1_.13, ...), custom_call_target="tpu_custom_call", output_to_operand_aliasing={{1}: (8, {}), {2}: (9, {}), {3}: (10, {}), {4}: (11, {})} | custom-call | tf_op jit(solution)/shard_map/layer_forward/pallas_call | solution.py:306
  91.8 15.0 %layer_forward.6 = (f32[456,512]{1,0:T(8,128)}, f32[2,3,456,512]{3,2,1,0:T(8,128)}, f32[2,2,456,1536]{3,2,1,0:T(8,128)}, f32[2,2,456,512]{3,2,1,0:T(8,128)}, f32[2,456,2048]{2,1,0:T(8,128)}) custom-call(s32[3]{0:T(128)} %get-tuple-element.119.refs_0_, s32[2]{0:T(128)} %refs_1_.13, ...), custom_call_target="tpu_custom_call", output_to_operand_aliasing={{1}: (8, {}), {2}: (9, {}), {3}: (10, {}), {4}: (11, {})} | custom-call | tf_op jit(solution)/shard_map/layer_forward/pallas_call | solution.py:306
  106.8 7.3 %layer_backward.3 = (f32[456,512]{1,0:T(8,128)}, f32[3,512]{1,0:T(4,128)}, f32[2,3,456,512]{3,2,1,0:T(8,128)}, f32[2,2,456,1536]{3,2,1,0:T(8,128)}, f32[2,3,456,...) custom-call(s32[3]{0:T(128)} %get-tuple-element.119.refs_0_, s32[2]{0:T(128)} %refs_1_.13, ...), custom_call_target="tpu_custom_call" | custom-call | tf_op jit(solution)/shard_map/layer_backward/pallas_call | solution.py:352
  118.0 70.3 %collective-permute-done.2.refs_3_ = f32[456,512]{1,0:T(8,128)S(1)} collective-permute-done((f32[456,512]{1,0:T(8,128)}, f32[456,512]{1,0:T(8,128)S(1)}, u32[]{:S(2)}, u32[]{:S(2)}) %collective-permute-start.2) | collective-permute-done | bytes 933920 | tf_op jit(solution)/shard_map/ppermute | solution.py:423
  189.2 44.7 %layer_backward.4 = (f32[456,512]{1,0:T(8,128)}, f32[3,512]{1,0:T(4,128)}, f32[2,3,456,512]{3,2,1,0:T(8,128)}, f32[2,2,456,1536]{3,2,1,0:T(8,128)}, f32[2,3,456,...) custom-call(s32[3]{0:T(128)} %get-tuple-element.116.refs_0_, ...), custom_call_target="tpu_custom_call", output_to_operand_aliasing={{2}: (12, {}), {3}: (13, {}), {4}: (14, {}), {5}: (15, {}),... | custom-call | tf_op jit(solution)/shard_map/layer_backward/pallas_call | solution.py:352
  235.2 36.3 %collective-permute-done.3.refs_2_.refs_3_ = f32[456,512]{1,0:T(8,128)S(1)} collective-permute-done((f32[456,512]{1,0:T(8,128)}, f32[456,512]{1,0:T(8,128)S(1)}, u32[]{:S(2)}, u32[]{:S(2)}) %collective-permute-start.3) | collective-permute-done | bytes 933920 | tf_op jit(solution)/shard_map/ppermute | solution.py:426
  272.4 44.7 %layer_backward.5 = (f32[456,512]{1,0:T(8,128)}, f32[3,512]{1,0:T(4,128)}, f32[2,3,456,512]{3,2,1,0:T(8,128)}, f32[2,2,456,1536]{3,2,1,0:T(8,128)}, f32[2,3,456,...) custom-call(s32[3]{0:T(128)} %get-tuple-element.117.refs_0_, ...), custom_call_target="tpu_custom_call", output_to_operand_aliasing={{2}: (12, {}), {3}: (13, {}), {4}: (14, {}), {5}: (15, {}),... | custom-call | tf_op jit(solution)/shard_map/layer_backward/pallas_call | solution.py:352
  317.1 4.1 fusion.33
  321.3 3.6 fusion.38
  324.9 9.7 %fusion.6 = f32[1,512,1536]{2,1,0:T(8,128)} fusion(f32[2,2,456,1536]{3,2,1,0:T(8,128)} %get-tuple-element.85, f32[2,3,456,512]{3,2,1,0:T(8,128)S(1)} %copy-done.1), kind=kOutput, calls=%fused_computation.7 | convolution fusion | flops 4303355904 | bytes 10616832 | tf_op jit(solution)/shard_map/tck,tcn->kn/dot_general | solution.py:436
  334.7 7.3 %fusion.9 = f32[1,512,1536]{2,1,0:T(8,128)} fusion(f32[2,2,456,1536]{3,2,1,0:T(8,128)S(1)} %bitcast.104, f32[2,3,456,512]{3,2,1,0:T(8,128)S(1)} %copy-done.1), kind=kOutput, calls=%fused_computation.8 | convolution fusion | flops 4303355904 | bytes 10616832 | tf_op jit(solution)/shard_map/tck,tcn->kn/dot_general | solution.py:436
  342.0 17.0 %convolution_bitcast_fusion = f32[1,2048,512]{2,1,0:T(8,128)} fusion(f32[2,456,2048]{2,1,0:T(8,128)S(1)} %bitcast.106, f32[2,3,456,512]{3,2,1,0:T(8,128)} %get-tuple-element.87), kind=kOutput, calls=%fused_computation.9 | convolution fusion | flops 5737807872 | bytes 13533184 | tf_op jit(solution)/shard_map/tck,tcn->kn/dot_general | solution.py:436
  359.1 9.0 %convolution_bitcast_fusion.1 = f32[1,512,2048]{2,1,0:T(8,128)} fusion(f32[2,456,2048]{2,1,0:T(8,128)S(1)} %bitcast.108, f32[2,3,456,512]{3,2,1,0:T(8,128)S(1)} %copy-done.1), kind=kOutput, calls=%fused_computation.10 | convolution fusion | flops 5737807872 | bytes 13533184 | tf_op jit(solution)/shard_map/tck,tcn->kn/dot_general | solution.py:436
  370.7 3.3 maximum_bitcast_fusion
  378.7 2.4 stack.66
  385.9 2.4 stack.80
  388.2 2.4 stack.69
  391.9 35.9 %psum.42 = f32[1,3,512]{2,1,0:T(4,128)S(1)} all-reduce(f32[1,3,512]{2,1,0:T(4,128)} %select_bitcast_fusion), channel_id=1, replica_groups=mesh['section'=2,'dp'=16] {'dp'}, use_global_device_ids=true, to_apply=%region_0.1 | all-reduce | flops 1536 | bytes 12288 | tf_op jit(solution)/shard_map/psum | solution.py:447
  428.4 4.0 maximum_select_fusion
  437.6 38.4 %psum.47 = f32[512]{0:T(512)} all-reduce(f32[512]{0:T(512)S(1)} %broadcast_select_fusion), channel_id=1, replica_groups=mesh['section'=2,'dp'=16] {'section','dp'}, use_global_device_ids=true, to_apply=%region_6.7 | all-reduce | flops 512 | bytes 4096 | tf_op jit(solution)/shard_map/psum | solution.py:448
  476.0 200.2 %all-reduce.3.cloned.1.call-done = (f32[1,2,512,1536]{3,2,1,0:T(8,128)}, f32[1,2,512,512]{3,2,1,0:T(8,128)}, f32[1,512,2048]{2,1,0:T(8,128)}, f32[1,2048,512]{2,1,0:T(8,128)}) async-done(((f32[1,2,512,1536]{3,2,1,0:T(8,128)}, f32[1,2,512,512]{3,2,1,0:T(8,128)}, f32[1,512,2048]{2,1,0:T(8,128)}, f32[1,2048,512]{2,1,0:T(8,128)}), (f32[1,2,512,1536]{3,2,1,0:T(8,128)}, f32[1,2,512,512]{3,2,1,0:T(8,128)}, ...) | async-done | bytes 16777232 | tf_op jit(solution)/shard_map/psum | solution.py:447
  676.2 6.1 copy.111
  (93 shorter events, 47.4 us)
Async XLA Ops:
  7.2 669.1 %all-reduce.3.cloned.1.call-start = ((), (), s32[]{:S(2)}) async-start(), calls=%async_computation | async-start | bytes 33554432 | tf_op jit(solution)/shard_map/psum | solution.py:447
  13.2 37.8 %copy-start.15 = (s32[3]{0:T(128)S(1)}, s32[3]{0:T(128)}, u32[]{:S(2)}) copy-start(s32[3]{0:T(128)} %constant.22.clone) | copy-start | bytes 40
  13.2 37.8 %copy-start.16 = (s32[3]{0:T(128)S(1)}, s32[3]{0:T(128)}, u32[]{:S(2)}) copy-start(s32[3]{0:T(128)} %constant.23.clone) | copy-start | bytes 40
  47.7 44.1 %collective-permute-start = (f32[456,512]{1,0:T(8,128)}, f32[456,512]{1,0:T(8,128)}, u32[]{:S(2)}, u32[]{:S(2)}) collective-permute-start(f32[456,512]{1,0:T(8,128)} %get-tuple-element.49), channel_id=1, source_target_pairs={{0,16},{1,17},{2,18},{3,19},{4,20},{5,21},{6,22},{7,23},{8,24},{9,... | collective-permute-start | bytes 2801672 | tf_op jit(solution)/shard_map/ppermute | solution.py:418
  86.4 30.7 %collective-permute-start.1 = (f32[456,512]{1,0:T(8,128)}, f32[456,512]{1,0:T(8,128)}, u32[]{:S(2)}, u32[]{:S(2)}) collective-permute-start(f32[456,512]{1,0:T(8,128)} %get-tuple-element.54), channel_id=1, source_target_pairs={{0,16},{1,17},{2,18},{3,19},{4,20},{5,21},{6,22},{7,23},{8,24},{9,... | collective-permute-start | bytes 2801672 | tf_op jit(solution)/shard_map/ppermute | solution.py:420
  114.1 74.2 %collective-permute-start.2 = (f32[456,512]{1,0:T(8,128)}, f32[456,512]{1,0:T(8,128)S(1)}, u32[]{:S(2)}, u32[]{:S(2)}) collective-permute-start(f32[456,512]{1,0:T(8,128)} %get-tuple-element.65), channel_id=1, source_target_pairs={{16,0},{17,1},{18,2},{19,3},{20,4},{21,5},{22,6},{23,7},{24,8},{25... | collective-permute-start | bytes 2801672 | tf_op jit(solution)/shard_map/ppermute | solution.py:423
  233.9 37.6 %collective-permute-start.3 = (f32[456,512]{1,0:T(8,128)}, f32[456,512]{1,0:T(8,128)S(1)}, u32[]{:S(2)}, u32[]{:S(2)}) collective-permute-start(f32[456,512]{1,0:T(8,128)} %get-tuple-element.74), channel_id=1, source_target_pairs={{16,0},{17,1},{18,2},{19,3},{20,4},{21,5},{22,6},{23,7},{24,8},{25... | collective-permute-start | bytes 2801672 | tf_op jit(solution)/shard_map/ppermute | solution.py:426
  317.1 4.2 copy-start
  317.1 7.8 %copy-start.1 = (f32[2,3,456,512]{3,2,1,0:T(8,128)S(1)}, f32[2,3,456,512]{3,2,1,0:T(8,128)}, u32[]{:S(2)}) copy-start(f32[2,3,456,512]{3,2,1,0:T(8,128)} %get-tuple-element.84) | copy-start | bytes 16809988
  321.3 13.4 %slice-start = ((s8[11206656]{0:T(1024)(128)(4,1)}), s8[4194304]{0:T(1024)(128)(4,1)S(1)}, s32[]{:S(2)}) async-start(s8[11206656]{0:T(1024)(128)(4,1)} %bitcast.103), calls=%async_computation.1 | async-start | bytes 8388608
  324.9 9.7 %slice-start.1 = ((s8[11206656]{0:T(1024)(128)(4,1)}), s8[4194304]{0:T(1024)(128)(4,1)S(1)}, s32[]{:S(2)}) async-start(s8[11206656]{0:T(1024)(128)(4,1)} %bitcast.103), calls=%async_computation.2 | async-start | bytes 8388608
  324.9 9.7 %slice-start.2 = ((s8[11206656]{0:T(1024)(128)(4,1)}), s8[2818048]{0:T(1024)(128)(4,1)S(1)}, s32[]{:S(2)}) async-start(s8[11206656]{0:T(1024)(128)(4,1)} %bitcast.103), calls=%async_computation.3 | async-start | bytes 5636096
  324.9 17.1 %slice-start.3 = ((s8[7471104]{0:T(1024)(128)(4,1)}), s8[4194304]{0:T(1024)(128)(4,1)S(1)}, s32[]{:S(2)}) async-start(s8[7471104]{0:T(1024)(128)(4,1)} %bitcast.105), calls=%async_computation.4 | async-start | bytes 8388608
  334.6 7.4 %slice-start.4 = ((s8[7471104]{0:T(1024)(128)(4,1)}), s8[3276800]{0:T(1024)(128)(4,1)S(1)}, s32[]{:S(2)}) async-start(s8[7471104]{0:T(1024)(128)(4,1)} %bitcast.105), calls=%async_computation.5 | async-start | bytes 6553600
  334.6 24.4 %slice-start.5 = ((s8[7471104]{0:T(1024)(128)(4,1)}), s8[4194304]{0:T(1024)(128)(4,1)S(1)}, s32[]{:S(2)}) async-start(s8[7471104]{0:T(1024)(128)(4,1)} %bitcast.107), calls=%async_computation.6 | async-start | bytes 8388608
  342.0 17.0 %slice-start.6 = ((s8[7471104]{0:T(1024)(128)(4,1)}), s8[3276800]{0:T(1024)(128)(4,1)S(1)}, s32[]{:S(2)}) async-start(s8[7471104]{0:T(1024)(128)(4,1)} %bitcast.107), calls=%async_computation.7 | async-start | bytes 6553600
  359.1 10.5 %copy-start.8 = (f32[1,512,1536]{2,1,0:T(8,128)S(1)}, f32[1,512,1536]{2,1,0:T(8,128)}, u32[]{:S(2)}) copy-start(f32[1,512,1536]{2,1,0:T(8,128)} %fusion.9) | copy-start | bytes 9437188
  368.0 2.6 copy-start.7
  374.1 3.3 copy-start.6
  378.7 2.4 copy-start.12
  385.9 4.8 copy-start.13
  676.2 6.1 copy-start.9
  682.3 2.9 copy-start.4
  685.3 3.7 copy-start.3
  (6 other events, 8.8 us)
Sparse Core Ops, SparseCore 0:
  374.2 302.0 all-reduce.2

commit v2 on v0

v2 whole, which is shorter than its diff:
```python
import functools
from types import SimpleNamespace

import jax
import jax.numpy as jnp
from jax import lax
from jax.experimental import pallas as pl
from jax.experimental.pallas import tpu as pltpu
from jax.sharding import PartitionSpec as P

HEADS = 4
EPSILON = 1e-05
NEG = -1e30
INV_SQRT2 = 0.7071067811865476
INV_SQRT2PI = 0.3989422804014327
VMEM_LIMIT = 62 * 1024 * 1024
TILE = 512
F32, BF16 = jnp.float32, jnp.bfloat16


def dot(a, b, contract=((1,), (0,))):
    return lax.dot_general(a, b, (contract, ((), ())), preferred_element_type=F32)


def split(v):
    hi = v.astype(BF16)
    return hi, (v - hi.astype(F32)).astype(BF16)


def put(ref, index, v):
    hi, lo = split(v)
    ref[(0, *index)] = hi
    ref[(1, *index)] = lo


def parts(ref, *index):
    return ref[(0, *index)], ref[(1, *index)]


def wide(a, b, ca, cb):
    (ah, al), (bh, bl) = a, b
    return dot(jnp.concatenate([ah, ah, al], ca), jnp.concatenate([bh, bl, bh], cb), ((ca,), (cb,)))


def side(a, b):
    (ah, al), (bh, bl) = a, b
    width = bh.shape[1]
    both = dot(ah, jnp.concatenate([bh, bl], 1))
    return both[:, :width] + both[:, width:] + dot(al, bh)


def normalized(h):
    centred = h - jnp.mean(h, axis=-1, keepdims=True)
    rstd = lax.rsqrt(jnp.mean(centred * centred, axis=-1, keepdims=True) + EPSILON)
    return centred * rstd, rstd


def norm_back(n, rstd, gain, da):
    dn = da * gain
    return rstd * (dn - jnp.mean(dn, axis=-1, keepdims=True) - n * jnp.mean(dn * n, axis=-1, keepdims=True))


def cell_ids(start, count, rows, along):
    shape = (count, 1) if along == 0 else (1, count)
    at = lax.broadcasted_iota(jnp.int32, shape, along) + start
    feat = lax.shift_right_logical(at * ((1 << 20) // rows + 1), 20)
    return at - feat * rows, feat


def up16(n):
    return (n + 15) // 16 * 16


def col_blocks(rows, feat):
    cells = up16(rows * feat)
    half = up16((feat + 1) // 2 * rows)
    first_keys = min(cells, up16((((half - 1) // rows) + 1) * rows))
    second_keys = ((half // rows) * rows) // 16 * 16
    return (((0, half), (0, first_keys)), ((half, cells), (second_keys, cells)))


def lanes(j, width):
    return pl.ds(pl.multiple_of(j * width, width), width)


def start(src, dst, sem):
    copy = pltpu.make_async_copy(src, dst, sem)
    copy.start()
    return copy


def attention_biases(rows, feat, context, col_refs, row_ref, keys_along):
    for ((q0, q1), (k0, k1)), ref in zip(col_blocks(rows, feat), col_refs):
        _, q_feat = cell_ids(q0, q1 - q0, rows, 1 - keys_along)
        k_row, k_feat = cell_ids(k0, k1 - k0, rows, keys_along)
        ref[...] = jnp.where((q_feat == k_feat) & (k_row < context), 0.0, NEG)
    cells = up16(rows * feat)
    q_row, _ = cell_ids(0, cells, rows, 1 - keys_along)
    k_row, k_feat = cell_ids(0, cells, rows, keys_along)
    row_ref[...] = jnp.where((q_row == k_row) & (k_feat < feat), 0.0, NEG)


def phi_of(z):
    return 0.5 * (1.0 + lax.erf(z * INV_SQRT2))


SMEM, VMEM, ANY = pltpu.SMEM, pltpu.VMEM, pl.ANY


def call(name, body, ins, outs, carried, scratch):
    held = {k: v for k, v in carried.items() if not isinstance(v, jax.ShapeDtypeStruct)}
    names = [*ins, *("_" + k for k in held), *outs, *carried, *scratch]

    def kernel(*refs):
        body(SimpleNamespace(**dict(zip(names, refs))))

    first_carried = len(outs)
    order = list(carried)
    results = pl.pallas_call(
        kernel,
        out_shape=[t for t, _ in outs.values()] + [jax.ShapeDtypeStruct(v.shape, v.dtype) for v in carried.values()],
        in_specs=[pl.BlockSpec(memory_space=s) for _, s in ins.values()] + [pl.BlockSpec(memory_space=ANY)] * len(held),
        out_specs=[pl.BlockSpec(memory_space=s) for _, s in outs.values()]
        + [pl.BlockSpec(memory_space=ANY)] * len(carried),
        input_output_aliases={len(ins) + i: first_carried + order.index(k) for i, k in enumerate(held)},
        scratch_shapes=list(scratch.values()),
        compiler_params=pltpu.CompilerParams(vmem_limit_bytes=VMEM_LIMIT),
        name=name,
    )(*(a for a, _ in ins.values()), *held.values())
    return SimpleNamespace(**dict(zip([*outs, *carried], results)))


def f32(*shape):
    return jax.ShapeDtypeStruct(shape, F32)


def b16(*shape):
    return jax.ShapeDtypeStruct(shape, BF16)


def dma(n):
    return pltpu.SemaphoreType.DMA((n,))


class Layer:
    def __init__(self, tables, rows, feat, width, ff):
        self.tables, self.rows, self.feat, self.width, self.ff = tables, rows, feat, width, ff
        self.cells = up16(rows * feat)
        self.hd = width // HEADS
        self.scale = self.hd ** (-0.5)

    def bias_scratch(self, keys_along):
        def shape(q, k):
            return (k, q) if keys_along == 0 else (q, k)

        out = {}
        for name, ((q0, q1), (k0, k1)) in zip(("bias_a", "bias_b"), col_blocks(self.rows, self.feat)):
            out[name] = VMEM(shape(q1 - q0, k1 - k0), F32)
        out["bias_row"] = VMEM((self.cells, self.cells), F32)
        return out

    def sites(self, r, site):
        if site == 1:
            return list(zip(col_blocks(self.rows, self.feat), (r.bias_a, r.bias_b)))
        return [(((0, self.cells), (0, self.cells)), r.bias_row)]

    def forward(self, kind, ctl, ctx, x, extra, gains, weights, saved):
        t, c, w, ff = self.tables, self.cells, self.width, self.ff
        splitting = weights is None
        ins = {"ctl": (ctl, SMEM), "ctx": (ctx, SMEM), "x": (x, ANY), "gains": (gains, VMEM)}
        if kind == "cells":
            ins |= {"mask": (extra.mask, VMEM), "embed": (extra.embed, VMEM)}
        names = ("win", "wout", "wup", "wdown")
        raw = extra.raw
        shapes = [(2, *a.shape) for a in raw]
        for n, a in zip(names, raw if splitting else weights):
            ins[n] = (a, ANY)
        outs = {"y": (f32(self.rows * self.feat, w), ANY)}
        if splitting:
            outs |= {n + "_out": (b16(*s), ANY) for n, s in zip(names, shapes)}
        if saved is None:
            saved = {
                "out": f32(t, self.rows * self.feat, w),
                "hs": f32(t, 3, c, w),
                "qkvs": b16(t, 2, 2, c, 3 * w),
                "os": b16(t, 2, 2, c, w),
                "zs": f32(t, c, ff),
            }
        scratch = {n + "_v": VMEM(s, BF16) for n, s in zip(names, shapes)}
        scratch |= {
            "h_v": VMEM((3, c, w), F32),
            "qkv_v": VMEM((2, 2, c, 3 * w), BF16),
            "o_v": VMEM((2, 2, c, w), BF16),
            "z_v": VMEM((c, ff), F32),
            "g_v": VMEM((2, c, ff), BF16),
            "a_v": VMEM((2, c, w), BF16),
            "y_v": VMEM((c, w), F32),
            "sem_in": dma(5),
            "sem_out": dma(14),
        } | self.bias_scratch(1)
        if splitting:
            scratch |= {n + "_raw": VMEM(a.shape, F32) for n, a in zip(names, raw)}

        def body(r):
            vs = [getattr(r, n + "_v") for n in names]
            kept = []
            if splitting:
                raws = [getattr(r, n + "_raw") for n in names]
                loads = [start(getattr(r, n), v, r.sem_in.at[1 + i]) for i, (n, v) in enumerate(zip(names, raws))]
                for i, n in enumerate(names):
                    loads[i].wait()
                    split_weights(raws[i], vs[i])
                    kept.append(start(vs[i], getattr(r, n + "_out"), r.sem_out.at[10 + i]))

            @pl.when(r.ctl[0] == 1)
            def _():
                if splitting:
                    waits = [lambda: None] * 4
                else:
                    waits = [start(getattr(r, n), v, r.sem_in.at[1 + i]).wait for i, (n, v) in enumerate(zip(names, vs))]
                self.forward_body(r, kind, waits)

            for copy in kept:
                copy.wait()

        res = call("layer_forward", body, ins, outs, saved, scratch)
        if splitting:
            weights = [getattr(res, n + "_out") for n in names]
        return res.y, weights, {k: getattr(res, k) for k in saved}

    def forward_body(self, r, kind, waits):
        rows, feat, c, w, ff, hd = self.rows, self.feat, self.cells, self.width, self.ff, self.hd
        table = r.ctl[1]
        stores = []

        def keep(src, dst):
            stores.append(start(src, dst, r.sem_out.at[len(stores)]))

        real = rows * feat
        x = r.x if kind == "flat" else r.x.at[table]
        load_x = start(x, r.h_v.at[0, 0:real], r.sem_in.at[0])
        attention_biases(rows, feat, r.ctx[table], (r.bias_a, r.bias_b), r.bias_row, 1)
        r.h_v[0, real:, :] = jnp.zeros((c - real, w), F32)
        load_x.wait()
        if kind != "flat":
            r.h_v[0] = jnp.where(r.mask[table] == 1.0, r.embed[...], r.h_v[0])
        keep(r.h_v.at[0], r.hs.at[table, 0])
        for site in range(2):
            put(r.a_v, (), normalized(r.h_v[site])[0] * r.gains[site : site + 1, :])
            if site == 0:
                waits[0]()

            @pl.loop(0, 3 * w // TILE)
            def _(j):
                at = lanes(j, TILE)
                out = wide(parts(r.a_v), parts(r.win_v, site, slice(None), at), 1, 0)
                put(r.qkv_v, (site, slice(None), at), out)

            keep(r.qkv_v.at[:, site], r.qkvs.at[table, :, site])

            @pl.loop(0, HEADS)
            def _(head):
                for ((q0, q1), (k0, k1)), bias in self.sites(r, site):
                    q = parts(r.qkv_v, site, slice(q0, q1), lanes(head, hd))
                    k = parts(r.qkv_v, site, slice(k0, k1), lanes(HEADS + head, hd))
                    v = parts(r.qkv_v, site, slice(k0, k1), lanes(2 * HEADS + head, hd))
                    s = wide(q, k, 1, 1) * self.scale + bias[...]
                    e = jnp.exp(s - jnp.max(s, axis=-1, keepdims=True))
                    p = e * (1.0 / jnp.sum(e, axis=-1, keepdims=True))
                    put(r.o_v, (site, slice(q0, q1), lanes(head, hd)), side(split(p), v))

            keep(r.o_v.at[:, site], r.os.at[table, :, site])
            if site == 0:
                waits[1]()
            r.h_v[site + 1] = r.h_v[site] + wide(parts(r.o_v, site), parts(r.wout_v, site), 1, 0)
            keep(r.h_v.at[site + 1], r.hs.at[table, site + 1])
        put(r.a_v, (), normalized(r.h_v[2])[0] * r.gains[2:3, :])
        waits[2]()

        @pl.loop(0, ff // TILE)
        def _(j):
            at = lanes(j, TILE)
            z = wide(parts(r.a_v), parts(r.wup_v, slice(None), at), 1, 0)
            r.z_v[:, at] = z
            put(r.g_v, (slice(None), at), z * phi_of(z))

        keep(r.z_v, r.zs.at[table])
        waits[3]()
        r.y_v[...] = r.h_v[2]

        @pl.loop(0, ff // TILE)
        def _(j):
            at = lanes(j, TILE)
            r.y_v[...] += wide(parts(r.g_v, slice(None), at), parts(r.wdown_v, at), 1, 0)

        keep(r.y_v.at[0:real], r.y)
        keep(r.y_v.at[0:real], r.out.at[table])
        for copy in stores:
            copy.wait()

    def mlp_back(self, ctl, cot, dy, gains, weights, saved, kept):
        t, c, w, ff = self.tables, self.cells, self.width, self.ff
        rows, feat = self.rows, self.feat
        ins = {"ctl": (ctl, SMEM), "gains": (gains, VMEM), "wup": (weights[2], ANY), "wdown": (weights[3], ANY)}
        ins |= {"hs": (saved["hs"], ANY), "zs": (saved["zs"], ANY), "dy": (dy, ANY)}
        if cot is not None:
            ins["cot"] = (cot, ANY)
        if kept is None:
            kept = {
                "dys": b16(t, 2, c, w),
                "gs": b16(t, 2, c, ff),
                "dzs": b16(t, 2, c, ff),
                "a2s": b16(t, 2, c, w),
            }
        outs = {"dw": (f32(c, w), ANY), "dgain": (f32(1, w), VMEM)}
        scratch = {
            "wup_v": VMEM(weights[2].shape, BF16),
            "wdown_v": VMEM(weights[3].shape, BF16),
            "w_v": VMEM((c, w), F32),
            "dy_v": VMEM((c, w), F32),
            "da_v": VMEM((c, w), F32),
            "z_v": VMEM((c, ff), F32),
            "dys_v": VMEM((2, c, w), BF16),
            "g_v": VMEM((2, c, ff), BF16),
            "dz_v": VMEM((2, c, ff), BF16),
            "a_v": VMEM((2, c, w), BF16),
            "sem_in": dma(5),
            "sem_out": dma(5),
        }

        def body(r):
            @pl.when(r.ctl[0] == 1)
            def _():
                table, real = r.ctl[1], rows * feat
                r.dy_v[real:, :] = jnp.zeros((c - real, w), F32)
                c_down = start(r.wdown, r.wdown_v, r.sem_in.at[1])
                c_z = start(r.zs.at[table], r.z_v, r.sem_in.at[2])
                c_up = start(r.wup, r.wup_v, r.sem_in.at[3])
                c_w = start(r.hs.at[table, 2], r.w_v, r.sem_in.at[4])
                if cot is not None:

                    @pl.when(r.ctl[2] == 0)
                    def _():
                        start(r.cot.at[table], r.dy_v.at[0:real], r.sem_in.at[0]).wait()

                @pl.when(r.ctl[2] == 1)
                def _():
                    start(r.dy, r.dy_v.at[0:real], r.sem_in.at[0]).wait()

                put(r.dys_v, (), r.dy_v[...])
                stores = [start(r.dys_v, r.dys.at[table], r.sem_out.at[0])]
                c_down.wait()
                c_z.wait()

                @pl.loop(0, ff // TILE)
                def _(j):
                    at = lanes(j, TILE)
                    dg = wide(parts(r.dys_v), parts(r.wdown_v, at), 1, 1)
                    z = r.z_v[:, at]
                    phi = phi_of(z)
                    put(r.g_v, (slice(None), at), z * phi)
                    put(r.dz_v, (slice(None), at), dg * (phi + z * (INV_SQRT2PI * jnp.exp(-0.5 * z * z))))

                stores.append(start(r.g_v, r.gs.at[table], r.sem_out.at[1]))
                stores.append(start(r.dz_v, r.dzs.at[table], r.sem_out.at[2]))
                c_up.wait()
                r.da_v[...] = jnp.zeros((c, w), F32)

                @pl.loop(0, ff // TILE)
                def _(j):
                    at = lanes(j, TILE)
                    r.da_v[...] += wide(parts(r.dz_v, slice(None), at), parts(r.wup_v, slice(None), at), 1, 1)

                c_w.wait()
                gain = r.gains[2:3, :]
                n, rstd = normalized(r.w_v[...])
                put(r.a_v, (), n * gain)
                stores.append(start(r.a_v, r.a2s.at[table], r.sem_out.at[3]))
                da = r.da_v[...]
                r.dgain[...] = jnp.sum(da * n, axis=0, keepdims=True)
                r.dy_v[...] += norm_back(n, rstd, gain, da)
                stores.append(start(r.dy_v, r.dw, r.sem_out.at[4]))
                for copy in stores:
                    copy.wait()

        res = call("mlp_backward", body, ins, outs, kept, scratch)
        return res.dw, res.dgain, {k: getattr(res, k) for k in kept}

    def attn_back(self, ctl, ctx, dw, mask, gains, weights, saved, kept):
        t, c, w = self.tables, self.cells, self.width
        rows, feat, hd = self.rows, self.feat, self.hd
        ins = {"ctl": (ctl, SMEM), "ctx": (ctx, SMEM), "dw": (dw, ANY), "mask": (mask, VMEM), "gains": (gains, VMEM)}
        ins |= {"win": (weights[0], ANY), "wout": (weights[1], ANY), "hs": (saved["hs"], ANY), "qkvs": (saved["qkvs"], ANY)}
        if kept is None:
            kept = {
                "din": f32(t, rows * feat, w),
                "as_": b16(t, 2, 2, c, w),
                "dqkvs": b16(t, 2, 2, c, 3 * w),
                "dhs": b16(t, 2, 2, c, w),
            }
        outs = {"dx": (f32(rows * feat, w), ANY), "small": (f32(3, w), VMEM)}
        scratch = {
            "win_v": VMEM(weights[0].shape, BF16),
            "wout_v": VMEM(weights[1].shape, BF16),
            "h_v": VMEM((2, c, w), F32),
            "dh_v": VMEM((c, w), F32),
            "da_v": VMEM((c, w), F32),
            "qkv_v": VMEM((2, 2, c, 3 * w), BF16),
            "dqkv_v": VMEM((2, 2, c, 3 * w), BF16),
            "dqkv_f": VMEM((c, 3 * w), F32),
            "do_v": VMEM((2, c, w), BF16),
            "dhs_v": VMEM((2, 2, c, w), BF16),
            "a_v": VMEM((2, 2, c, w), BF16),
            "sem_in": dma(5),
            "sem_out": dma(8),
        } | self.bias_scratch(0)

        def body(r):
            @pl.when(r.ctl[0] == 1)
            def _():
                table, real = r.ctl[1], rows * feat
                c_dw = start(r.dw, r.dh_v, r.sem_in.at[0])
                c_wout = start(r.wout, r.wout_v, r.sem_in.at[1])
                c_qkv = start(r.qkvs.at[table], r.qkv_v, r.sem_in.at[2])
                c_win = start(r.win, r.win_v, r.sem_in.at[3])
                c_h = start(r.hs.at[table, 0:2], r.h_v, r.sem_in.at[4])
                stores = []

                def keep(src, dst):
                    stores.append(start(src, dst, r.sem_out.at[len(stores)]))

                attention_biases(rows, feat, r.ctx[table], (r.bias_a, r.bias_b), r.bias_row, 0)
                c_dw.wait()
                for site in (1, 0):
                    put(r.dhs_v, (site,), r.dh_v[...])
                    keep(r.dhs_v.at[:, site], r.dhs.at[table, :, site])
                    if site == 1:
                        c_wout.wait()
                    put(r.do_v, (), wide(parts(r.dhs_v, site), parts(r.wout_v, site), 1, 1))
                    if site == 1:
                        c_qkv.wait()

                    @pl.loop(0, HEADS)
                    def _(head):
                        done = 0
                        at_q, at_k, at_v = lanes(head, hd), lanes(HEADS + head, hd), lanes(2 * HEADS + head, hd)
                        for ((q0, q1), (k0, k1)), bias in self.sites(r, site):
                            q = parts(r.qkv_v, site, slice(q0, q1), at_q)
                            k = parts(r.qkv_v, site, slice(k0, k1), at_k)
                            v = parts(r.qkv_v, site, slice(k0, k1), at_v)
                            do = parts(r.do_v, slice(q0, q1), at_q)
                            s = wide(k, q, 1, 1) * self.scale + bias[...]
                            e = jnp.exp(s - jnp.max(s, axis=0, keepdims=True))
                            p = e * (1.0 / jnp.sum(e, axis=0, keepdims=True))
                            dp = wide(v, do, 1, 1)
                            ds = split(p * (dp - jnp.sum(p * dp, axis=0, keepdims=True)) * self.scale)
                            r.dqkv_f[q0:q1, at_q] = wide(tuple(x.T for x in k), ds, 1, 0).T
                            for at, term in ((at_k, side(ds, q)), (at_v, side(split(p), do))):
                                if done > k0:
                                    r.dqkv_f[k0:done, at] += term[: done - k0]
                                    r.dqkv_f[done:k1, at] = term[done - k0 :]
                                else:
                                    r.dqkv_f[k0:k1, at] = term
                            done = k1

                    if site == 1:
                        c_win.wait()
                    r.da_v[...] = jnp.zeros((c, w), F32)

                    @pl.loop(0, 3 * w // TILE)
                    def _(j):
                        at = lanes(j, TILE)
                        d = split(r.dqkv_f[:, at])
                        r.dqkv_v[0, site, :, at] = d[0]
                        r.dqkv_v[1, site, :, at] = d[1]
                        r.da_v[...] += wide(d, parts(r.win_v, site, slice(None), at), 1, 1)

                    keep(r.dqkv_v.at[:, site], r.dqkvs.at[table, :, site])
                    if site == 1:
                        c_h.wait()
                    gain = r.gains[site : site + 1, :]
                    n, rstd = normalized(r.h_v[site])
                    put(r.a_v, (site,), n * gain)
                    keep(r.a_v.at[:, site], r.as_.at[table, :, site])
                    da = r.da_v[...]
                    r.small[site : site + 1, :] = jnp.sum(da * n, axis=0, keepdims=True)
                    r.dh_v[...] += norm_back(n, rstd, gain, da)
                keep(r.dh_v.at[0:real], r.dx)
                missing = r.mask[table] == 1.0
                r.small[2:3, :] = jnp.sum(jnp.where(missing, r.dh_v[...], 0.0), axis=0, keepdims=True)
                r.da_v[...] = jnp.where(missing, 0.0, r.dh_v[...])
                keep(r.da_v.at[0:real], r.din.at[table])
                for copy in stores:
                    copy.wait()

        res = call("attention_backward", body, ins, outs, kept, scratch)
        return res.dx, res.small, {k: getattr(res, k) for k in kept}


def split_weights(raw, v):
    step = 64
    lead = raw.shape[:-2]
    for at in [(s,) for s in range(lead[0])] if lead else [()]:

        @pl.loop(0, raw.shape[-2] // step)
        def _(j):
            block = pl.ds(pl.multiple_of(j * step, step), step)
            put(v, (*at, block), raw[(*at, block)])


def weight_grad(a, b, site=None):
    t, c = a.shape[0], a.shape[-2]
    k, n = a.shape[-1], b.shape[-1]
    sites = 1 if a.ndim == 4 else a.shape[2]
    lead = () if a.ndim == 4 else (1,)
    tile = 256

    def kernel(a_ref, b_ref, out_ref):
        mid = (0,) * len(lead)

        def ends(ref, at):
            return [(ref[(i, 0, *mid, slice(None), at)], ref[(i, 1, *mid, slice(None), at)]) for i in range(t)]

        left = ends(a_ref, slice(None))

        @pl.loop(0, n // TILE)
        def _(j):
            at = lanes(j, TILE)
            total = None
            for (ah, al), (bh, bl) in zip(left, ends(b_ref, at)):
                term = dot(jnp.concatenate([ah, ah, al], 0), jnp.concatenate([bh, bl, bh], 0), ((0,), (0,)))
                total = term if total is None else total + term
            out_ref[(*mid, slice(None), at)] = total

    def spec(block, index):
        return pl.BlockSpec(block, index)

    if lead:
        a_spec = spec((t, 2, 1, c, tile), lambda s, i: (0, 0, s, 0, i))
        b_spec = spec((t, 2, 1, c, n), lambda s, i: (0, 0, s, 0, 0))
        o_spec = spec((1, tile, n), lambda s, i: (s, i, 0))
        shape = f32(sites, k, n)
    else:
        a_spec = spec((t, 2, c, tile), lambda s, i: (0, 0, 0, i))
        b_spec = spec((t, 2, c, n), lambda s, i: (0, 0, 0, 0))
        o_spec = spec((tile, n), lambda s, i: (i, 0))
        shape = f32(k, n)
    return pl.pallas_call(
        kernel,
        grid=(sites, k // tile),
        in_specs=[a_spec, b_spec],
        out_specs=o_spec,
        out_shape=shape,
        compiler_params=pltpu.CompilerParams(vmem_limit_bytes=VMEM_LIMIT),
        cost_estimate=pl.CostEstimate(flops=6 * sites * t * c * k * n, bytes_accessed=4 * sites * (t * c * (k + n) + k * n), transcendentals=0),
        name="weight_gradient",
    )(a, b)


def local(
    cells,
    missing_mask,
    missing_embed,
    context_rows,
    norm_gains,
    attn_in,
    attn_out,
    mlp_up,
    mlp_down,
    cotangent,
):
    section = lax.axis_index("section")
    tables, rows, feat, width = cells.shape
    layer = Layer(tables, rows, feat, width, mlp_up.shape[2])
    gains = norm_gains[0]
    is_first = section == 0

    def flat(tables_of_cells):
        return jnp.swapaxes(tables_of_cells, 1, 2).reshape(tables, rows * feat, -1)

    def unflat(cells_of_tables):
        return jnp.swapaxes(cells_of_tables.reshape(tables, feat, rows, width), 1, 2)

    cells, cotangent = flat(cells), flat(cotangent)
    flat_mask = flat(missing_mask == 1)
    flat_mask = jnp.pad(flat_mask, ((0, 0), (0, layer.cells - rows * feat), (0, 0)))
    mask = flat_mask.astype(F32)
    mask_here = jnp.where(is_first, mask, 0.0)

    def ctl(at_first, at_last):
        return jnp.where(is_first, jnp.array(at_first, jnp.int32), jnp.array(at_last, jnp.int32))

    idle = (0, 0, 0)
    fwd_pairs, bwd_pairs = [(0, 1)], [(1, 0)]
    extra = SimpleNamespace(mask=mask, embed=missing_embed[None], raw=(attn_in[0], attn_out[0], mlp_up[0], mlp_down[0]))

    def forward(kind, control, x, weights, saved):
        return layer.forward(kind, control, context_rows, x, extra, gains, weights, saved)

    def mlp_back(control, cot, dy, kept):
        return layer.mlp_back(control, cot, dy, gains, weights, saved, kept)

    def attn_back(control, dw, kept):
        return layer.attn_back(control, context_rows, dw, mask_here, gains, weights, saved, kept)

    y0, weights, saved = forward("cells", ctl((1, 0, 0), idle), cells, None, None)
    r0 = lax.ppermute(y0, "section", fwd_pairs)
    y1, _, saved = forward("cells", ctl((1, 1, 0), idle), cells, weights, saved)
    r1 = lax.ppermute(y1, "section", fwd_pairs)
    _, _, saved = forward("flat", ctl(idle, (1, 0, 0)), r0, weights, saved)
    dw0, dg0, kept_m = mlp_back(ctl(idle, (1, 0, 0)), cotangent, r0, None)
    d0, small0, kept_a = attn_back(ctl(idle, (1, 0, 0)), dw0, None)
    e0 = lax.ppermute(d0, "section", bwd_pairs)
    _, _, saved = forward("flat", ctl(idle, (1, 1, 0)), r1, weights, saved)
    dw1, dg1, kept_m = mlp_back(ctl((1, 0, 1), (1, 1, 0)), cotangent, e0, kept_m)
    d1, small1, kept_a = attn_back(ctl((1, 0, 0), (1, 1, 0)), dw1, kept_a)
    e1 = lax.ppermute(d1, "section", bwd_pairs)
    dw2, dg2, kept_m = mlp_back(ctl((1, 1, 1), idle), None, e1, kept_m)
    d_up = weight_grad(kept_m["a2s"], kept_m["dzs"])
    d_down = weight_grad(kept_m["gs"], kept_m["dys"])
    up_all, down_all = lax.psum((d_up, d_down), "dp")
    _, small2, kept_a = attn_back(ctl((1, 1, 0), idle), dw2, kept_a)
    d_in = weight_grad(kept_a["as_"], kept_a["dqkvs"])
    d_out = weight_grad(saved["os"], kept_a["dhs"])

    def row(first_a, first_b, last_a, last_b):
        return jnp.where(is_first, first_a + first_b, last_a + last_b)

    d_small = jnp.concatenate(
        [
            row(small1[0:2], small2[0:2], small0[0:2], small1[0:2]),
            row(dg1, dg2, dg0, dg1),
            jnp.where(is_first, small1[2:3] + small2[2:3], 0.0),
            jnp.zeros((4, width), F32),
        ],
        0,
    )
    d_rest = jnp.concatenate([d_out.reshape(2 * width, width), d_small], 0)
    (d_in, d_rest), up_all, down_all = lax.optimization_barrier(((d_in, d_rest), up_all, down_all))
    in_all, rest_all = lax.psum((d_in, d_rest), "dp")
    out_all = rest_all[: 2 * width].reshape(2, width, width)
    gain_all = rest_all[2 * width : 2 * width + 3]
    missing = rest_all[2 * width + 3]
    missing_all = jnp.where(is_first, missing, lax.ppermute(missing, "section", fwd_pairs))
    return (
        unflat(saved["out"])[None],
        unflat(kept_a["din"])[None],
        gain_all[None],
        in_all[None],
        out_all[None],
        up_all[None],
        down_all[None],
        missing_all,
    )


def solution(mesh):
    in_specs = (
        P("dp", None, None, None),
        P("dp", None, None),
        P(),
        P("dp"),
        P("section", None, None),
        P("section", None, None, None),
        P("section", None, None, None),
        P("section", None, None),
        P("section", None, None),
        P("dp", None, None, None),
    )
    out_specs = (
        P("section", "dp", None, None, None),
        P("section", "dp", None, None, None),
        P("section", None, None),
        P("section", None, None, None),
        P("section", None, None, None),
        P("section", None, None),
        P("section", None, None),
        P(),
    )
    return jax.shard_map(local, mesh=mesh, in_specs=in_specs, out_specs=out_specs, check_vma=False)
```

time: 1250 us -> 685 us (0.55)
  matrix products: 346 us -> 0 us
  Pallas kernels: 0 us -> 220 us
  local copies, waits for them, and re-layouts: 154 us -> 28.5 us
  other arithmetic: 122 us -> 5.71 us
  blocking collectives: 77.1 us -> 0 us
  starting transfers between devices: 84.2 us -> 8.72 us
  loops' own time: 26.8 us -> 0 us
  waiting for transfers between devices: 427 us -> 401 us
    dot_general x78 -> x0, matrix products: 346 us -> none  [the longest x46 261 us: project(): return jnp.einsum('rfd,de->rfe', inputs, matrix, precision=exact_mode)]
    pallas_call x0 -> x14, Pallas kernels: none -> 220 us  [the longest x10 170 us: call(): pl.pallas_call(kernel, out_shape=[t for t, _ in outs.values()] + [jax.Sha...]
    ppermute x6 -> x5, waiting for transfers between devices: 207 us -> 116 us  [the longest x1 68.2 us: local(): e0 = lax.ppermute(d0, 'section', bwd_pairs)]
    psum x2 -> x0, blocking collectives: 77.1 us -> none  [the longest x1 42.3 us: local(): missing_grad = lax.psum(partial_missing, ('section', 'dp'))]
    ppermute x6 -> x5, starting transfers between devices: 84.2 us -> 8.64 us  [the longest x1 3.36 us: local(): lax.ppermute(missing, 'section', fwd_pairs)]
    psum x1 -> x2, waiting for transfers between devices: 220 us -> 285 us  [the longest x1 175 us: local(): in_all, rest_all = lax.psum((d_in, d_rest), 'dp')]
    add x17 -> x0, other arithmetic: 56.9 us -> none  [the longest x15 56.9 us: backward_moment(): totals = tuple((total + term for total, term in zip(totals, terms)))]
    reshape x28 -> x1, local copies, waits for them, and re-layouts: 49.9 us -> 0.23 us  [flat(): return jnp.swapaxes(tables_of_cells, 1, 2).reshape(tables, rows * feat, -1)]
  transfers between devices with their start and end apart: 7 -> 7, of which waited for: 6 -> 5; matrix products, arithmetic and copies ran while one was open for 6% -> 2% of each run, Pallas kernels for 0% -> 14%
where the time goes in v2:
time: 685 us; the launch traced here: 679 us
  waiting for transfers between devices  401 us (59%)
  Pallas kernels  220 us (32%)
  local copies, waits for them, and re-layouts  28.5 us (4%)
  between operations  14.7 us (2%)
  starting transfers between devices  8.72 us (1%)
    psum x1, waiting for transfers between devices, local(): in_all, rest_all = lax.psum((d_in, d_rest), 'dp')  175 us
    pallas_call x10, Pallas kernels, call(): pl.pallas_call(kernel, out_shape=[t for t, _ in outs.values()] + [jax.Sha...  170 us
    psum x1, waiting for transfers between devices, local(): up_all, down_all = lax.psum((d_up, d_down), 'dp')  109 us
    ppermute x1, waiting for transfers between devices, local(): e0 = lax.ppermute(d0, 'section', bwd_pairs)  68.2 us
    pallas_call x4, Pallas kernels, weight_grad(): pl.pallas_call(kernel, grid=(sites, k // tile), in_specs=[a_spec, b_spec]...  50.3 us
    ppermute x1, waiting for transfers between devices, local(): e1 = lax.ppermute(d1, 'section', bwd_pairs)  34.3 us
    unnamed x26, local copies, waits for them, and re-layouts  16.4 us
  transfers between devices with their start and end apart: 7, of which 5 were waited for; matrix products, arithmetic and copies ran while one was open for 2% of the time, Pallas kernels for 14%

profile of v2, /device:TPU:0, one launch (start us, length us, event | category | flops | bytes accessed | tf_op | source)
XLA Modules:
  0.0 678.5 jit_solution(13195748052470480768)
XLA Ops:
  11.6 37.8 %layer_forward.4 = (f32[456,512]{1,0:T(8,128)}, bf16[2,2,512,1536]{3,2,1,0:T(8,128)(2,1)}, bf16[2,2,512,512]{3,2,1,0:T(8,128)(2,1)}, bf16[2,512,2048]{2,1,0:T(8,...) custom-call(s32[3]{0:T(128)} %get-tuple-element.146.refs_0_, ...), custom_call_target="tpu_custom_call" | custom-call | tf_op jit(solution)/shard_map/layer_forward/pallas_call | solution.py:119
  50.8 33.6 %layer_forward.5 = (f32[456,512]{1,0:T(8,128)}, f32[2,456,512]{2,1,0:T(8,128)}, f32[2,3,464,512]{3,2,1,0:T(8,128)}, bf16[2,2,2,464,1536]{4,3,2,1,0:T(8,128)(2,1)...) custom-call(s32[3]{0:T(128)} %get-tuple-element.143.refs_0_, ...), custom_call_target="tpu_custom_call", output_to_operand_aliasing={{1}: (10, {}), {2}: (11, {}), {3}: (12, {}), {4}: (13, {}),... | custom-call | tf_op jit(solution)/shard_map/layer_forward/pallas_call | solution.py:119
  88.6 1.8 mlp_backward.3
  90.4 1.8 attention_backward.3
  93.4 13.5 %collective-permute-done.refs_2_ = f32[456,512]{1,0:T(8,128)S(1)} collective-permute-done((f32[456,512]{1,0:T(8,128)}, f32[456,512]{1,0:T(8,128)S(1)}, u32[]{:S(2)}, u32[]{:S(2)}) %collective-permute-start) | collective-permute-done | bytes 933920 | tf_op jit(solution)/shard_map/ppermute | solution.py:609
  109.0 68.2 %collective-permute-done.2.refs_6_ = f32[456,512]{1,0:T(8,128)S(1)} collective-permute-done((f32[456,512]{1,0:T(8,128)}, f32[456,512]{1,0:T(8,128)S(1)}, u32[]{:S(2)}, u32[]{:S(2)}) %collective-permute-start.2) | collective-permute-done | bytes 933920 | tf_op jit(solution)/shard_map/ppermute | solution.py:613
  178.1 17.7 %mlp_backward.4 = (f32[464,512]{1,0:T(8,128)}, f32[1,512]{1,0:T(1,128)}, bf16[2,2,464,512]{3,2,1,0:T(8,128)(2,1)}, bf16[2,2,464,2048]{3,2,1,0:T(8,128)(2,1)}, bf...) custom-call(s32[3]{0:T(128)} %get-tuple-element.142.refs_0_, ...), custom_call_target="tpu_custom_call", output_to_operand_aliasing={{2}: (8, {}), {3}: (9, {}), {4}: (10, {}), {5}: (11, {})} | custom-call | tf_op jit(solution)/shard_map/mlp_backward/pallas_call | solution.py:119
  195.8 28.7 %attention_backward.4 = (f32[456,512]{1,0:T(8,128)}, f32[3,512]{1,0:T(4,128)}, f32[2,456,512]{2,1,0:T(8,128)}, bf16[2,2,2,464,512]{4,3,2,1,0:T(8,128)(2,1)}, bf1...) custom-call(s32[3]{0:T(128)} %get-tuple-element.145.refs_0_, ...), custom_call_target="tpu_custom_call", output_to_operand_aliasing={{2}: (9, {}), {3}: (10, {}), {4}: (11, {}), {5}: (12, {})} | custom-call | tf_op jit(solution)/shard_map/attention_backward/pallas_call | solution.py:119
  225.8 34.3 %collective-permute-done.3.refs_6_ = f32[456,512]{1,0:T(8,128)S(1)} collective-permute-done((f32[456,512]{1,0:T(8,128)}, f32[456,512]{1,0:T(8,128)S(1)}, u32[]{:S(2)}, u32[]{:S(2)}) %collective-permute-start.3) | collective-permute-done | bytes 933920 | tf_op jit(solution)/shard_map/ppermute | solution.py:617
  261.1 18.0 %mlp_backward.5 = (f32[464,512]{1,0:T(8,128)}, f32[1,512]{1,0:T(1,128)}, bf16[2,2,464,512]{3,2,1,0:T(8,128)(2,1)}, bf16[2,2,464,2048]{3,2,1,0:T(8,128)(2,1)}, bf...) custom-call(s32[3]{0:T(128)} %broadcast.9.refs_0_, ...), custom_call_target="tpu_custom_call", output_to_operand_aliasing={{2}: (7, {}), {3}: (8, {}), {4}: (9, {}), {5}: (10, {})} | custom-call | tf_op jit(solution)/shard_map/mlp_backward/pallas_call | solution.py:119
  279.1 12.1 %weight_gradient.7 = f32[2048,512]{1,0:T(8,128)} custom-call(bf16[2,2,464,2048]{3,2,1,0:T(8,128)(2,1)} %get-tuple-element.132.a_ref, bf16[2,2,464,512]{3,2,1,0:T(8,128)(2,1)} %get-tuple-element.133.b_ref), custom_call_target="tpu_custom_call" | custom-call | flops 5838471168 | bytes 13697024 | tf_op jit(solution)/shard_map/weight_gradient/pallas_call | solution.py:548
  291.2 13.1 %weight_gradient.6 = f32[512,2048]{1,0:T(8,128)} custom-call(bf16[2,2,464,512]{3,2,1,0:T(8,128)(2,1)} %get-tuple-element.130.a_ref, bf16[2,2,464,2048]{3,2,1,0:T(8,128)(2,1)} %get-tuple-element.131.b_ref), custom_call_target="tpu_custom_call" | custom-call | flops 5838471168 | bytes 13697024 | tf_op jit(solution)/shard_map/weight_gradient/pallas_call | solution.py:548
  304.4 28.5 %attention_backward.5 = (f32[456,512]{1,0:T(8,128)}, f32[3,512]{1,0:T(4,128)}, f32[2,456,512]{2,1,0:T(8,128)}, bf16[2,2,2,464,512]{4,3,2,1,0:T(8,128)(2,1)}, bf1...) custom-call(s32[3]{0:T(128)} %get-tuple-element.143.refs_0_, ...), custom_call_target="tpu_custom_call", output_to_operand_aliasing={{2}: (9, {}), {3}: (10, {}), {4}: (11, {}), {5}: (12, {})} | custom-call | tf_op jit(solution)/shard_map/attention_backward/pallas_call | solution.py:119
  334.4 8.0 %weight_gradient.5 = f32[2,512,512]{2,1,0:T(8,128)} custom-call(bf16[2,2,2,464,512]{4,3,2,1,0:T(8,128)(2,1)} %get-tuple-element.122.a_ref, bf16[2,2,2,464,512]{4,3,2,1,0:T(8,128)(2,1)} %get-tuple-element.123.b_ref), custom_call_target="tpu_custom_call" | custom-call | flops 2919235584 | bytes 9699328 | tf_op jit(solution)/shard_map/weight_gradient/pallas_call | solution.py:548
  342.4 6.2 concatenate.3
  348.6 17.2 %weight_gradient.4 = f32[2,512,1536]{2,1,0:T(8,128)} custom-call(bf16[2,2,2,464,512]{4,3,2,1,0:T(8,128)(2,1)} %get-tuple-element.120.a_ref, bf16[2,2,2,464,1536]{4,3,2,1,0:T(8,128)(2,1)} %get-tuple-element.121.b_ref), custom_call_target="tpu_custom_call" | custom-call | flops 8757706752 | bytes 21495808 | tf_op jit(solution)/shard_map/weight_gradient/pallas_call | solution.py:548
  365.8 109.5 %all-reduce.8.cloned.1.call-done = (f32[512,2048]{1,0:T(8,128)}, f32[2048,512]{1,0:T(8,128)}) async-done(((f32[512,2048]{1,0:T(8,128)}, f32[2048,512]{1,0:T(8,128)}), (f32[512,2048]{1,0:T(8,128)}, f32[2048,512]{1,0:T(8,128)})) %all-reduce.8.cloned.1.call-update) | async-done | bytes 8388624 | tf_op jit(solution)/shard_map/psum | solution.py:621
  475.3 175.1 %all-reduce.6.cloned.1.call-done = (f32[1032,512]{1,0:T(8,128)}, f32[1,2,512,1536]{3,2,1,0:T(8,128)}) async-done(((f32[1032,512]{1,0:T(8,128)}, f32[1,2,512,1536]{3,2,1,0:T(8,128)}), (f32[1032,512]{1,0:T(8,128)}, f32[1,2,512,1536]{3,2,1,0:T(8,128)})) %all-reduce.6.cloned.1.call-update) | async-done | bytes 8405008 | tf_op jit(solution)/shard_map/psum | solution.py:640
  651.1 3.4 collective-permute-start.4
  654.5 3.1 slice.34
  659.4 6.1 copy.110
  665.5 2.1 copy.111
  667.7 1.6 copy-done
  669.2 2.0 copy.112
  (48 shorter events, 20.6 us)
Async XLA Ops:
  7.2 468.1 %all-reduce.8.cloned.1.call-start = ((), (), s32[]{:S(2)}) async-start(), calls=%async_computation.1 | async-start | bytes 16777216 | tf_op jit(solution)/shard_map/psum | solution.py:621
  49.4 37.2 %collective-permute-start.1 = (f32[456,512]{1,0:T(8,128)}, f32[456,512]{1,0:T(8,128)S(1)}, u32[]{:S(2)}, u32[]{:S(2)}) collective-permute-start(f32[456,512]{1,0:T(8,128)} %get-tuple-element.83), channel_id=1, source_target_pairs={{0,16},{1,17},{2,18},{3,19},{4,20},{5,21},{6,22},{7,23},{8,24},{9,... | collective-permute-start | bytes 2801672 | tf_op jit(solution)/shard_map/ppermute | solution.py:607
  84.4 22.5 %collective-permute-start = (f32[456,512]{1,0:T(8,128)}, f32[456,512]{1,0:T(8,128)S(1)}, u32[]{:S(2)}, u32[]{:S(2)}) collective-permute-start(f32[456,512]{1,0:T(8,128)} %get-tuple-element.82), channel_id=1, source_target_pairs={{0,16},{1,17},{2,18},{3,19},{4,20},{5,21},{6,22},{7,23},{8,24},{9,... | collective-permute-start | bytes 2801672 | tf_op jit(solution)/shard_map/ppermute | solution.py:609
  86.6 0.9 copy-start.2
  92.1 85.0 %collective-permute-start.2 = (f32[456,512]{1,0:T(8,128)}, f32[456,512]{1,0:T(8,128)S(1)}, u32[]{:S(2)}, u32[]{:S(2)}) collective-permute-start(f32[456,512]{1,0:T(8,128)} %get-tuple-element.98), channel_id=1, source_target_pairs={{16,0},{17,1},{18,2},{19,3},{20,4},{21,5},{22,6},{23,7},{24,8},{25... | collective-permute-start | bytes 2801672 | tf_op jit(solution)/shard_map/ppermute | solution.py:613
  106.9 0.9 copy-start.4
  177.2 1.0 copy-start.3
  224.5 35.6 %collective-permute-start.3 = (f32[456,512]{1,0:T(8,128)}, f32[456,512]{1,0:T(8,128)S(1)}, u32[]{:S(2)}, u32[]{:S(2)}) collective-permute-start(f32[456,512]{1,0:T(8,128)} %get-tuple-element.109), channel_id=1, source_target_pairs={{16,0},{17,1},{18,2},{19,3},{20,4},{21,5},{22,6},{23,7},{24,8},{25... | collective-permute-start | bytes 2801672 | tf_op jit(solution)/shard_map/ppermute | solution.py:617
  260.2 1.0 copy-start.5
  304.3 346.1 %all-reduce.6.cloned.1.call-start = ((), (), s32[]{:S(2)}) async-start(), calls=%async_computation | async-start | bytes 16809984 | tf_op jit(solution)/shard_map/psum | solution.py:640
  304.3 28.6 %copy-start.6 = (f32[3,512]{1,0:T(4,128)S(1)}, f32[3,512]{1,0:T(4,128)}, u32[]{:S(2)}) copy-start(f32[3,512]{1,0:T(4,128)} %get-tuple-element.124) | copy-start | bytes 18436
  304.3 28.6 %copy-start.8 = (f32[1,512]{1,0:T(1,128)S(1)}, f32[1,512]{1,0:T(1,128)}, u32[]{:S(2)}) copy-start(f32[1,512]{1,0:T(1,128)} %get-tuple-element.129) | copy-start | bytes 6148
  304.3 28.6 %copy-start.9 = (f32[1,512]{1,0:T(1,128)S(1)}, f32[1,512]{1,0:T(1,128)}, u32[]{:S(2)}) copy-start(f32[1,512]{1,0:T(1,128)} %get-tuple-element.127) | copy-start | bytes 6148
  304.4 28.6 %copy-start.10 = (f32[1,512]{1,0:T(1,128)S(1)}, f32[1,512]{1,0:T(1,128)}, u32[]{:S(2)}) copy-start(f32[1,512]{1,0:T(1,128)} %get-tuple-element.128) | copy-start | bytes 6148
  304.4 29.3 %copy-start.7 = (f32[3,512]{1,0:T(4,128)S(1)}, f32[3,512]{1,0:T(4,128)}, u32[]{:S(2)}) copy-start(f32[3,512]{1,0:T(4,128)} %get-tuple-element.126) | copy-start | bytes 18436
  651.1 7.8 %collective-permute-start.4 = (f32[512]{0:T(512)S(1)}, f32[512]{0:T(512)S(1)}, u32[]{:S(2)}, u32[]{:S(2)}) collective-permute-start(f32[512]{0:T(512)S(1)} %bitcast.59), channel_id=1, source_target_pairs={{0,16},{1,17},{2,18},{3,19},{4,20},{5,21},{6,22},{7,23},{8,24},{9,... | collective-permute-start | bytes 6152 | tf_op jit(solution)/shard_map/ppermute | solution.py:644
  659.4 6.1 copy-start.1
  665.5 3.7 copy-start
Sparse Core Ops, SparseCore 0:
  304.4 170.8 all-reduce.7
  480.1 170.1 all-reduce.5

commit v3 on v2

--- a/solution.py
+++ b/solution.py
@@ -508,53 +508,304 @@
             put(v, (*at, block), raw[(*at, block)])
 
 
-def weight_grad(a, b, site=None):
-    t, c = a.shape[0], a.shape[-2]
-    k, n = a.shape[-1], b.shape[-1]
-    sites = 1 if a.ndim == 4 else a.shape[2]
-    lead = () if a.ndim == 4 else (1,)
-    tile = 256
-
-    def kernel(a_ref, b_ref, out_ref):
-        mid = (0,) * len(lead)
-
-        def ends(ref, at):
-            return [(ref[(i, 0, *mid, slice(None), at)], ref[(i, 1, *mid, slice(None), at)]) for i in range(t)]
-
-        left = ends(a_ref, slice(None))
-
-        @pl.loop(0, n // TILE)
+class GradSum:
+    BLOCK = 256
+    SLACK = 2
+    RING = 8
+
+    def __init__(self, count, tables, cells, width, ff):
+        self.count, self.tables, self.cells, self.width = count, tables, cells, width
+        self.rest = count // 4
+        shapes = [("gs", "dys", None, "down", ff, width), ("a2s", "dzs", None, "up", width, ff)]
+        for site in (1, 0):
+            shapes.append(("as_", "dqkvs", site, "win", width, 3 * width))
+            shapes.append(("os", "dhs", site, "wout", width, width))
+        self.groups, at = [], 0
+        for left, right, site, out, k, n in shapes:
+            blocks = (k // self.BLOCK) * (n // TILE)
+            self.groups.append((at, at + blocks, left, right, site, out, n // TILE))
+            at += blocks
+        self.blocks = at
+        self.per_chunk = max(1, 4 * self.rest * 8 // self.BLOCK)
+        self.chunks = self.blocks // self.per_chunk
+        self.rows = self.per_chunk * self.BLOCK
+
+    def select(self, q, action):
+        for group in self.groups:
+            first, stop, *_, across = group
+
+            @pl.when((q >= first) & (q < stop))
+            def _():
+                action(group, (q - first) // across, (q - first) % across)
+
+    def load(self, r, q):
+        slot = q % 2
+
+        def action(group, i, j):
+            _, _, left, right, site, _, _ = group
+            mid = () if site is None else (site,)
+            a, b = getattr(r, left), getattr(r, right)
+            for t in range(self.tables):
+                for part in range(2):
+                    sem = 2 * t + part
+                    at = (t, part, *mid, slice(None))
+                    start(a.at[(*at, lanes(i, self.BLOCK))], r.a_v.at[slot, t, part], r.a_sem.at[slot, sem])
+                    start(b.at[(*at, lanes(j, TILE))], r.b_v.at[slot, t, part], r.b_sem.at[slot, sem])
+
+        self.select(q, action)
+
+    def wait_load(self, r, slot):
+        for t in range(self.tables):
+            for part in range(2):
+                sem = 2 * t + part
+                a, b = r.a_v.at[slot, t, part], r.b_v.at[slot, t, part]
+                pltpu.make_async_copy(a, a, r.a_sem.at[slot, sem]).wait()
+                pltpu.make_async_copy(b, b, r.b_sem.at[slot, sem]).wait()
+
+    def product(self, r, q):
+        slot = q % 2
+        self.wait_load(r, slot)
+
+        @pl.when(q + 1 < self.blocks)
+        def _():
+            self.load(r, q + 1)
+
+        left, right = [], []
+        for t in range(self.tables):
+            (ah, al), (bh, bl) = parts(r.a_v.at[slot, t]), parts(r.b_v.at[slot, t])
+            left += [ah, ah, al]
+            right += [bh, bl, bh]
+        rows = pl.ds(pl.multiple_of(q % self.per_chunk * self.BLOCK, self.BLOCK), self.BLOCK)
+        r.sums[q // self.per_chunk % self.RING, rows] = dot(jnp.concatenate(left, 0), jnp.concatenate(right, 0), ((0,), (0,)))
+
+    def store(self, r, q):
+        def action(group, i, j):
+            _, _, _, _, site, out, _ = group
+            dst = getattr(r, out)
+            rows = pl.ds(pl.multiple_of(i * self.BLOCK, self.BLOCK), self.BLOCK)
+            dst = dst.at[rows, lanes(j, TILE)] if site is None else dst.at[site, rows, lanes(j, TILE)]
+            u = q % self.per_chunk
+            at = pl.ds(pl.multiple_of(u * self.BLOCK, self.BLOCK), self.BLOCK)
+            start(r.full.at[q // self.per_chunk, at], dst, r.store_sem.at[q // self.per_chunk % 2, u])
+
+        self.select(q, action)
+
+    def wait_store(self, r, c):
+        for u in range(self.per_chunk):
+            block = r.full.at[c, u * self.BLOCK : (u + 1) * self.BLOCK]
+            pltpu.make_async_copy(block, block, r.store_sem.at[c % 2, u]).wait()
+
+    def kernel(self, r):
+        count, rest, rows = self.count, self.rest, self.rows
+        half, quarter, piece = rows // 2, rows // 4, rows // 4 // rest
+        me, section = lax.axis_index("dp"), lax.axis_index("section")
+        core, pair, place = me % 2, me // 2 % 2, me // 4
+        sibling, neighbour = me + 1 - 2 * core, me + 2 - 4 * pair
+
+        def peer(j):
+            return lax.rem(place + j, rest) * 4 + me % 4
+
+        def span(at, size):
+            return pl.ds(pl.multiple_of(at, size), size)
+
+        mine = core * half
+        own = mine + pair * quarter
+        other = mine + (1 - pair) * quarter
+
+        def remote(src, dst, send, recv, device):
+            return pltpu.make_async_remote_copy(
+                src_ref=src, dst_ref=dst, send_sem=send, recv_sem=recv, device_id=device, device_id_type=pl.DeviceIdType.MESH
+            )
+
+        barrier = pltpu.get_barrier_semaphore()
+        pl.semaphore_signal(barrier, inc=1, device_id={"section": 1 - section}, device_id_type=pl.DeviceIdType.MESH)
+        for device in (sibling, neighbour):
+            pl.semaphore_signal(barrier, inc=1, device_id={"dp": device}, device_id_type=pl.DeviceIdType.MESH)
+
+        @pl.loop(1, rest)
         def _(j):
-            at = lanes(j, TILE)
-            total = None
-            for (ah, al), (bh, bl) in zip(left, ends(b_ref, at)):
-                term = dot(jnp.concatenate([ah, ah, al], 0), jnp.concatenate([bh, bl, bh], 0), ((0,), (0,)))
-                total = term if total is None else total + term
-            out_ref[(*mid, slice(None), at)] = total
-
-    def spec(block, index):
-        return pl.BlockSpec(block, index)
-
-    if lead:
-        a_spec = spec((t, 2, 1, c, tile), lambda s, i: (0, 0, s, 0, i))
-        b_spec = spec((t, 2, 1, c, n), lambda s, i: (0, 0, s, 0, 0))
-        o_spec = spec((1, tile, n), lambda s, i: (s, i, 0))
-        shape = f32(sites, k, n)
-    else:
-        a_spec = spec((t, 2, c, tile), lambda s, i: (0, 0, 0, i))
-        b_spec = spec((t, 2, c, n), lambda s, i: (0, 0, 0, 0))
-        o_spec = spec((tile, n), lambda s, i: (i, 0))
-        shape = f32(k, n)
-    return pl.pallas_call(
-        kernel,
-        grid=(sites, k // tile),
-        in_specs=[a_spec, b_spec],
-        out_specs=o_spec,
-        out_shape=shape,
-        compiler_params=pltpu.CompilerParams(vmem_limit_bytes=VMEM_LIMIT),
-        cost_estimate=pl.CostEstimate(flops=6 * sites * t * c * k * n, bytes_accessed=4 * sites * (t * c * (k + n) + k * n), transcendentals=0),
-        name="weight_gradient",
-    )(a, b)
+            pl.semaphore_signal(barrier, inc=1, device_id={"dp": peer(j)}, device_id_type=pl.DeviceIdType.MESH)
+
+        self.load(r, 0)
+        pl.semaphore_wait(barrier, rest + 2)
+
+        def halve(c):
+            src = r.sums.at[c % self.RING, span((1 - core) * half, half)]
+            return remote(src, r.got_half.at[c], r.send.at[0, c % self.RING], r.recv.at[0, c], {"dp": sibling})
+
+        def quarter_copy(c):
+            src = r.sums.at[c % self.RING, span(other, quarter)]
+            return remote(src, r.got_quarter.at[c], r.send.at[1, c % self.RING], r.recv.at[1, c], {"dp": neighbour})
+
+        def scatter(c, j):
+            src = r.sums.at[c % self.RING, span(own + lax.rem(place + j, rest) * piece, piece)]
+            dst = r.got_piece.at[c, j - 1]
+            return remote(src, dst, r.send_rest.at[0, c % self.RING, j - 1], r.recv_rest.at[0, c, j - 1], {"dp": peer(j)})
+
+        def gather(c, j):
+            at = r.full.at[c, span(own + place * piece, piece)]
+            return remote(at, at, r.send_rest.at[1, c % self.RING, j - 1], r.recv_rest.at[1, c, j - 1], {"dp": peer(j)})
+
+        def gather_quarter(c):
+            at = r.full.at[c, span(own, quarter)]
+            return remote(at, at, r.send.at[2, c % self.RING], r.recv.at[2, c], {"dp": neighbour})
+
+        def gather_half(c):
+            at = r.full.at[c, span(mine, half)]
+            return remote(at, at, r.send.at[3, c % self.RING], r.recv.at[3, c], {"dp": sibling})
+
+        def each(action):
+            pl.loop(1, rest)(action)
+
+        def after_halve(c):
+            halve(c).wait()
+            r.sums[c % self.RING, span(mine, half)] += r.got_half[c]
+            quarter_copy(c).start()
+
+        def after_quarter(c):
+            quarter_copy(c).wait()
+            r.sums[c % self.RING, span(own, quarter)] += r.got_quarter[c]
+            each(lambda j: scatter(c, j).start())
+
+        def after_scatter(c):
+            each(lambda j: scatter(c, j).wait())
+            total = r.sums[c % self.RING, span(own + place * piece, piece)]
+            for j in range(rest - 1):
+                total += r.got_piece[c, j]
+            r.full[c, span(own + place * piece, piece)] = total
+            each(lambda j: gather(c, j).start())
+
+        def after_gather(c):
+            each(lambda j: gather(c, j).wait())
+            gather_quarter(c).start()
+
+        def after_gather_quarter(c):
+            gather_quarter(c).wait()
+            gather_half(c).start()
+
+        def after_gather_half(c):
+            gather_half(c).wait()
+
+            @pl.when(c >= 2)
+            def _():
+                self.wait_store(r, c - 2)
+
+            @pl.loop(0, self.per_chunk)
+            def _(u):
+                self.store(r, c * self.per_chunk + u)
+
+        stages = [after_halve, after_quarter, after_scatter, after_gather, after_gather_quarter, after_gather_half]
+
+        def small_copy(k, device):
+            return remote(r.small_v.at[k], r.got_small.at[k], r.small_send.at[k], r.small_recv.at[k], device)
+
+        def small_rest(j):
+            dst = r.got_small.at[2 + j]
+            return remote(r.small_v.at[3], dst, r.small_send.at[2 + j], r.small_recv.at[2 + j], {"dp": peer(j)})
+
+        def small_step(step):
+            @pl.when(step == 0)
+            def _():
+                r.small_v[0] = r.small[...]
+                small_copy(0, {"section": 1 - section}).start()
+
+            @pl.when(step == 2)
+            def _():
+                small_copy(0, {"section": 1 - section}).wait()
+                row = lax.broadcasted_iota(jnp.int32, (8, self.width), 0)
+                r.small_v[1] = r.small_v[0] + jnp.where(row == 3, r.got_small[0], 0.0)
+                small_copy(1, {"dp": sibling}).start()
+
+            @pl.when(step == 4)
+            def _():
+                small_copy(1, {"dp": sibling}).wait()
+                r.small_v[2] = r.small_v[1] + r.got_small[1]
+                small_copy(2, {"dp": neighbour}).start()
+
+            @pl.when(step == 6)
+            def _():
+                small_copy(2, {"dp": neighbour}).wait()
+                r.small_v[3] = r.small_v[2] + r.got_small[2]
+                each(lambda j: small_rest(j).start())
+
+            @pl.when(step == 8)
+            def _():
+                each(lambda j: small_rest(j).wait())
+                total = r.small_v[3]
+                for j in range(1, rest):
+                    total += r.got_small[2 + j]
+                r.small_out[...] = total
+
+        @pl.loop(0, self.chunks + self.SLACK * len(stages))
+        def _(step):
+            for k in reversed(range(len(stages))):
+                c = step - self.SLACK * (k + 1)
+
+                @pl.when((c >= 0) & (c < self.chunks))
+                def _():
+                    stages[k](c)
+
+            small_step(step)
+
+            @pl.when(step < self.chunks)
+            def _():
+                @pl.loop(0, self.per_chunk)
+                def _(u):
+                    self.product(r, step * self.per_chunk + u)
+
+                halve(step).start()
+
+        for c in range(max(0, self.chunks - 2), self.chunks):
+            self.wait_store(r, c)
+
+    def __call__(self, operands, small):
+        t, cells, width = self.tables, self.cells, self.width
+        names = list(operands)
+        rest, chunks, rows = self.rest, self.chunks, self.rows
+        piece = rows // 4 // rest
+        ff = operands["gs"].shape[-1]
+        outs = {
+            "win": f32(2, width, 3 * width),
+            "wout": f32(2, width, width),
+            "up": f32(width, ff),
+            "down": f32(ff, width),
+            "small_out": f32(8, width),
+        }
+        scratch = {
+            "sums": VMEM((self.RING, rows, TILE), F32),
+            "full": VMEM((chunks, rows, TILE), F32),
+            "got_half": VMEM((chunks, rows // 2, TILE), F32),
+            "got_quarter": VMEM((chunks, rows // 4, TILE), F32),
+            "got_piece": VMEM((chunks, rest - 1, piece, TILE), F32),
+            "a_v": VMEM((2, t, 2, cells, self.BLOCK), BF16),
+            "b_v": VMEM((2, t, 2, cells, TILE), BF16),
+            "small_v": VMEM((4, 8, width), F32),
+            "got_small": VMEM((2 + rest, 8, width), F32),
+            "a_sem": pltpu.SemaphoreType.DMA((2, 2 * t)),
+            "b_sem": pltpu.SemaphoreType.DMA((2, 2 * t)),
+            "store_sem": pltpu.SemaphoreType.DMA((2, self.per_chunk)),
+            "send": pltpu.SemaphoreType.DMA((4, self.RING)),
+            "recv": pltpu.SemaphoreType.DMA((4, chunks)),
+            "send_rest": pltpu.SemaphoreType.DMA((2, self.RING, rest - 1)),
+            "recv_rest": pltpu.SemaphoreType.DMA((2, chunks, rest - 1)),
+            "small_send": pltpu.SemaphoreType.DMA((2 + rest,)),
+            "small_recv": pltpu.SemaphoreType.DMA((2 + rest,)),
+        }
+        refs = [*names, "small", *outs, *scratch]
+
+        def body(*args):
+            self.kernel(SimpleNamespace(**dict(zip(refs, args))))
+
+        results = pl.pallas_call(
+            body,
+            out_shape=list(outs.values()),
+            in_specs=[pl.BlockSpec(memory_space=ANY)] * len(names) + [pl.BlockSpec(memory_space=VMEM)],
+            out_specs=[pl.BlockSpec(memory_space=ANY)] * 4 + [pl.BlockSpec(memory_space=VMEM)],
+            scratch_shapes=list(scratch.values()),
+            compiler_params=pltpu.CompilerParams(vmem_limit_bytes=VMEM_LIMIT, collective_id=0, has_side_effects=True),
+            name="weight_gradient_sum",
+        )(*operands.values(), small)
+        return SimpleNamespace(**dict(zip(outs, results)))
 
 
 def local(
@@ -616,13 +867,7 @@
     d1, small1, kept_a = attn_back(ctl((1, 0, 0), (1, 1, 0)), dw1, kept_a)
     e1 = lax.ppermute(d1, "section", bwd_pairs)
     dw2, dg2, kept_m = mlp_back(ctl((1, 1, 1), idle), None, e1, kept_m)
-    d_up = weight_grad(kept_m["a2s"], kept_m["dzs"])
-    d_down = weight_grad(kept_m["gs"], kept_m["dys"])
-    up_all, down_all = lax.psum((d_up, d_down), "dp")
     _, small2, kept_a = attn_back(ctl((1, 1, 0), idle), dw2, kept_a)
-    d_in = weight_grad(kept_a["as_"], kept_a["dqkvs"])
-    d_out = weight_grad(saved["os"], kept_a["dhs"])
-
     def row(first_a, first_b, last_a, last_b):
         return jnp.where(is_first, first_a + first_b, last_a + last_b)
 
@@ -635,22 +880,18 @@
         ],
         0,
     )
-    d_rest = jnp.concatenate([d_out.reshape(2 * width, width), d_small], 0)
-    (d_in, d_rest), up_all, down_all = lax.optimization_barrier(((d_in, d_rest), up_all, down_all))
-    in_all, rest_all = lax.psum((d_in, d_rest), "dp")
-    out_all = rest_all[: 2 * width].reshape(2, width, width)
-    gain_all = rest_all[2 * width : 2 * width + 3]
-    missing = rest_all[2 * width + 3]
-    missing_all = jnp.where(is_first, missing, lax.ppermute(missing, "section", fwd_pairs))
+    operands = kept_m | kept_a | {"os": saved["os"]}
+    input_grads = operands.pop("din")
+    sums = GradSum(lax.axis_size("dp"), tables, layer.cells, width, mlp_up.shape[2])(operands, d_small)
     return (
         unflat(saved["out"])[None],
-        unflat(kept_a["din"])[None],
-        gain_all[None],
-        in_all[None],
-        out_all[None],
-        up_all[None],
-        down_all[None],
-        missing_all,
+        unflat(input_grads)[None],
+        sums.small_out[0:3][None],
+        sums.win[None],
+        sums.wout[None],
+        sums.up[None],
+        sums.down[None],
+        sums.small_out[3],
     )
 
 

time: 685 us -> 534 us (0.78)
  waiting for transfers between devices: 401 us -> 116 us
  Pallas kernels: 220 us -> 377 us
  between operations: 14.7 us -> 1.31 us
    psum x2 -> x0, waiting for transfers between devices: 285 us -> none  [the longest x1 175 us: local(): in_all, rest_all = lax.psum((d_in, d_rest), 'dp')]
    pallas_call x4 -> x1, Pallas kernels: 50.3 us -> 207 us  [__call__(): pl.pallas_call(body, out_shape=list(outs.values()), in_specs=[pl.BlockSpe...]
    unnamed x26 -> x30, local copies, waits for them, and re-layouts: 16.4 us -> 19.9 us
  transfers between devices with their start and end apart: 7 -> 4, of which waited for: 5 -> 3; matrix products, arithmetic and copies ran while one was open for 2% -> 0% of each run, Pallas kernels for 14% -> 7%
where the time goes in v3:
time: 534 us; the launch traced here: 528 us
  Pallas kernels  377 us (71%)
  waiting for transfers between devices  116 us (22%)
  local copies, waits for them, and re-layouts  22.7 us (4%)
  other arithmetic  5.8 us (1%)
    pallas_call x1, Pallas kernels, __call__(): pl.pallas_call(body, out_shape=list(outs.values()), in_specs=[pl.BlockSpe...  207 us
    pallas_call x10, Pallas kernels, call(): pl.pallas_call(kernel, out_shape=[t for t, _ in outs.values()] + [jax.Sha...  170 us
    ppermute x1, waiting for transfers between devices, local(): e0 = lax.ppermute(d0, 'section', bwd_pairs)  68.1 us
    ppermute x1, waiting for transfers between devices, local(): e1 = lax.ppermute(d1, 'section', bwd_pairs)  34.3 us
    unnamed x30, local copies, waits for them, and re-layouts  19.9 us
    ppermute x1, waiting for transfers between devices, local(): r1 = lax.ppermute(y1, 'section', fwd_pairs)  13.4 us
  transfers between devices with their start and end apart: 4, of which 3 were waited for; matrix products, arithmetic and copies ran while one was open for 0% of the time, Pallas kernels for 7%

profile of v3, /device:TPU:0, one launch (start us, length us, event | category | flops | bytes accessed | tf_op | source)
XLA Modules:
  0.0 527.6 jit_solution(965461231590154992)
XLA Ops:
  3.7 1.3 broadcast_select_fusion.4
  5.0 37.8 %layer_forward.4 = (f32[456,512]{1,0:T(8,128)}, bf16[2,2,512,1536]{3,2,1,0:T(8,128)(2,1)}, bf16[2,2,512,512]{3,2,1,0:T(8,128)(2,1)}, bf16[2,512,2048]{2,1,0:T(8,...) custom-call(s32[3]{0:T(128)} %get-tuple-element.160.refs_0_, ...), custom_call_target="tpu_custom_call" | custom-call | tf_op jit(solution)/shard_map/layer_forward/pallas_call | solution.py:119
  42.8 1.3 collective-permute-start.1
  44.2 33.6 %layer_forward.5 = (f32[456,512]{1,0:T(8,128)}, f32[2,456,512]{2,1,0:T(8,128)}, f32[2,3,464,512]{3,2,1,0:T(8,128)}, bf16[2,2,2,464,1536]{4,3,2,1,0:T(8,128)(2,1)...) custom-call(s32[3]{0:T(128)} %get-tuple-element.157.refs_0_, ...), custom_call_target="tpu_custom_call", output_to_operand_aliasing={{1}: (10, {}), {2}: (11, {}), {3}: (12, {}), {4}: (13, {}),... | custom-call | tf_op jit(solution)/shard_map/layer_forward/pallas_call | solution.py:119
  77.8 1.3 collective-permute-start
  82.0 1.8 mlp_backward.3
  83.8 1.8 attention_backward.3
  85.5 1.3 collective-permute-start.2
  86.8 13.4 %collective-permute-done.refs_2_ = f32[456,512]{1,0:T(8,128)S(1)} collective-permute-done((f32[456,512]{1,0:T(8,128)}, f32[456,512]{1,0:T(8,128)S(1)}, u32[]{:S(2)}, u32[]{:S(2)}) %collective-permute-start) | collective-permute-done | bytes 933920 | tf_op jit(solution)/shard_map/ppermute | solution.py:860
  102.4 68.1 %collective-permute-done.2.refs_6_ = f32[456,512]{1,0:T(8,128)S(1)} collective-permute-done((f32[456,512]{1,0:T(8,128)}, f32[456,512]{1,0:T(8,128)S(1)}, u32[]{:S(2)}, u32[]{:S(2)}) %collective-permute-start.2) | collective-permute-done | bytes 933920 | tf_op jit(solution)/shard_map/ppermute | solution.py:864
  171.5 17.6 %mlp_backward.4 = (f32[464,512]{1,0:T(8,128)}, f32[1,512]{1,0:T(1,128)}, bf16[2,2,464,512]{3,2,1,0:T(8,128)(2,1)}, bf16[2,2,464,2048]{3,2,1,0:T(8,128)(2,1)}, bf...) custom-call(s32[3]{0:T(128)} %get-tuple-element.156.refs_0_, ...), custom_call_target="tpu_custom_call", output_to_operand_aliasing={{2}: (8, {}), {3}: (9, {}), {4}: (10, {}), {5}: (11, {})} | custom-call | tf_op jit(solution)/shard_map/mlp_backward/pallas_call | solution.py:119
  189.1 28.7 %attention_backward.4 = (f32[456,512]{1,0:T(8,128)}, f32[3,512]{1,0:T(4,128)}, f32[2,456,512]{2,1,0:T(8,128)}, bf16[2,2,2,464,512]{4,3,2,1,0:T(8,128)(2,1)}, bf1...) custom-call(s32[3]{0:T(128)} %get-tuple-element.159.refs_0_, ...), custom_call_target="tpu_custom_call", output_to_operand_aliasing={{2}: (9, {}), {3}: (10, {}), {4}: (11, {}), {5}: (12, {})} | custom-call | tf_op jit(solution)/shard_map/attention_backward/pallas_call | solution.py:119
  217.8 1.3 collective-permute-start.3
  219.2 34.3 %collective-permute-done.3.refs_6_ = f32[456,512]{1,0:T(8,128)S(1)} collective-permute-done((f32[456,512]{1,0:T(8,128)}, f32[456,512]{1,0:T(8,128)S(1)}, u32[]{:S(2)}, u32[]{:S(2)}) %collective-permute-start.3) | collective-permute-done | bytes 933920 | tf_op jit(solution)/shard_map/ppermute | solution.py:868
  254.5 17.7 %mlp_backward.5 = (f32[464,512]{1,0:T(8,128)}, f32[1,512]{1,0:T(1,128)}, bf16[2,2,464,512]{3,2,1,0:T(8,128)(2,1)}, bf16[2,2,464,2048]{3,2,1,0:T(8,128)(2,1)}, bf...) custom-call(s32[3]{0:T(128)} %broadcast.9.refs_0_, ...), custom_call_target="tpu_custom_call", output_to_operand_aliasing={{2}: (7, {}), {3}: (8, {}), {4}: (9, {}), {5}: (10, {})} | custom-call | tf_op jit(solution)/shard_map/mlp_backward/pallas_call | solution.py:119
  272.3 28.8 %attention_backward.5 = (f32[456,512]{1,0:T(8,128)}, f32[3,512]{1,0:T(4,128)}, f32[2,456,512]{2,1,0:T(8,128)}, bf16[2,2,2,464,512]{4,3,2,1,0:T(8,128)(2,1)}, bf1...) custom-call(s32[3]{0:T(128)} %get-tuple-element.157.refs_0_, ...), custom_call_target="tpu_custom_call", output_to_operand_aliasing={{2}: (9, {}), {3}: (10, {}), {4}: (11, {}), {5}: (12, {})} | custom-call | tf_op jit(solution)/shard_map/attention_backward/pallas_call | solution.py:119
  303.2 206.6 %weight_gradient_sum.1 = (f32[2,512,1536]{2,1,0:T(8,128)}, f32[2,512,512]{2,1,0:T(8,128)}, f32[512,2048]{1,0:T(8,128)}, f32[2048,512]{1,0:T(8,128)}, f32[8,512]{1,0:T(8,128)}) custom-call(bf16[2,2,464,512]{3,2,1,0:T(8,128)(2,1)} %get-tuple-element.121.args_0_, bf16[2,2,464,2048]{3,2,1,0:T(8,128)(2,1)} %get-tuple-element.122.args_1_, ...), custom_call_target="tpu_custom_call" | custom-call | tf_op jit(solution)/shard_map/weight_gradient_sum/pallas_call | solution.py:799
  510.5 1.3 slice.28
  512.4 6.1 %copy.112 = f32[1,2,512,1536]{3,2,1,0:T(8,128)} copy(f32[1,2,512,1536]{3,2,1,0:T(8,128)} %bitcast.39) | data formatting | bytes 12582912
  518.5 1.3 copy.113
  519.8 1.6 copy-done.1
  521.4 2.1 copy.114
  523.6 1.6 copy-done
  525.1 2.0 copy.115
  (39 shorter events, 13.4 us)
Async XLA Ops:
  42.8 37.2 %collective-permute-start.1 = (f32[456,512]{1,0:T(8,128)}, f32[456,512]{1,0:T(8,128)S(1)}, u32[]{:S(2)}, u32[]{:S(2)}) collective-permute-start(f32[456,512]{1,0:T(8,128)} %get-tuple-element.84), channel_id=1, source_target_pairs={{0,16},{1,17},{2,18},{3,19},{4,20},{5,21},{6,22},{7,23},{8,24},{9,... | collective-permute-start | bytes 2801672 | tf_op jit(solution)/shard_map/ppermute | solution.py:858
  77.8 22.5 %collective-permute-start = (f32[456,512]{1,0:T(8,128)}, f32[456,512]{1,0:T(8,128)S(1)}, u32[]{:S(2)}, u32[]{:S(2)}) collective-permute-start(f32[456,512]{1,0:T(8,128)} %get-tuple-element.83), channel_id=1, source_target_pairs={{0,16},{1,17},{2,18},{3,19},{4,20},{5,21},{6,22},{7,23},{8,24},{9,... | collective-permute-start | bytes 2801672 | tf_op jit(solution)/shard_map/ppermute | solution.py:860
  80.0 0.9 copy-start.2
  85.5 85.0 %collective-permute-start.2 = (f32[456,512]{1,0:T(8,128)}, f32[456,512]{1,0:T(8,128)S(1)}, u32[]{:S(2)}, u32[]{:S(2)}) collective-permute-start(f32[456,512]{1,0:T(8,128)} %get-tuple-element.99), channel_id=1, source_target_pairs={{16,0},{17,1},{18,2},{19,3},{20,4},{21,5},{22,6},{23,7},{24,8},{25... | collective-permute-start | bytes 2801672 | tf_op jit(solution)/shard_map/ppermute | solution.py:864
  100.3 0.9 copy-start.5
  170.5 1.0 copy-start.4
  217.8 35.7 %collective-permute-start.3 = (f32[456,512]{1,0:T(8,128)}, f32[456,512]{1,0:T(8,128)S(1)}, u32[]{:S(2)}, u32[]{:S(2)}) collective-permute-start(f32[456,512]{1,0:T(8,128)} %get-tuple-element.110), channel_id=1, source_target_pairs={{16,0},{17,1},{18,2},{19,3},{20,4},{21,5},{22,6},{23,7},{24,8},{25... | collective-permute-start | bytes 2801672 | tf_op jit(solution)/shard_map/ppermute | solution.py:868
  253.5 1.0 copy-start.6
  272.2 28.8 %copy-start.7 = (f32[3,512]{1,0:T(4,128)S(1)}, f32[3,512]{1,0:T(4,128)}, u32[]{:S(2)}) copy-start(f32[3,512]{1,0:T(4,128)} %get-tuple-element.129) | copy-start | bytes 18436
  272.2 28.8 %copy-start.8 = (f32[3,512]{1,0:T(4,128)S(1)}, f32[3,512]{1,0:T(4,128)}, u32[]{:S(2)}) copy-start(f32[3,512]{1,0:T(4,128)} %get-tuple-element.131) | copy-start | bytes 18436
  272.3 29.5 %copy-start.9 = (f32[1,512]{1,0:T(1,128)S(1)}, f32[1,512]{1,0:T(1,128)}, u32[]{:S(2)}) copy-start(f32[1,512]{1,0:T(1,128)} %get-tuple-element.134) | copy-start | bytes 6148
  272.3 29.5 %copy-start.10 = (f32[1,512]{1,0:T(1,128)S(1)}, f32[1,512]{1,0:T(1,128)}, u32[]{:S(2)}) copy-start(f32[1,512]{1,0:T(1,128)} %get-tuple-element.132) | copy-start | bytes 6148
  272.3 29.5 %copy-start.11 = (f32[1,512]{1,0:T(1,128)S(1)}, f32[1,512]{1,0:T(1,128)}, u32[]{:S(2)}) copy-start(f32[1,512]{1,0:T(1,128)} %get-tuple-element.133) | copy-start | bytes 6148
  512.4 6.1 %copy-start.3 = (f32[2,512,512]{2,1,0:T(8,128)S(1)}, f32[2,512,512]{2,1,0:T(8,128)}, u32[]{:S(2)}) copy-start(f32[2,512,512]{2,1,0:T(8,128)} %get-tuple-element.137) | copy-start | bytes 6291460
  518.5 2.9 copy-start.1
  521.4 3.7 copy-start
